TPU v7x, 256 devices: a whole 4x4x8 slice. The times are simulated.
256 devices in a mesh: spec: 16 (over z, x_lo), line: 4 (over y), lay: 4 (over x_hi, core).
Axes of the slice: x: 4 (x_hi: 2, x_lo: 2; x = x_hi * 2 + x_lo), y: 4, z: 8, core: 2. Of those that a mesh axis runs over, the one named last changes fastest.
Arguments:
- line_offset: float32 [262144], P(('spec', 'line')), may hold values from 0 to 256
- line_strength: float32 [262144], P(('spec', 'line')), may hold values from 0.2 to 5
- lower_energy: float32 [262144], P(('spec', 'line')), may hold values from 20 to 2000
- lorentz_width: float32 [262144], P(('spec', 'line')), may hold values from 4 to 60
- doppler_width: float32 [262144], P(('spec', 'line')), may hold values from 2 to 12
- line_species: int32 [262144], P(('spec', 'line')), may hold values from 0 to 2
- cutoff: int32 [2048, 4], P(('spec', 'line')), may hold values from -1 to 255, as said below
- layer_pressure: float32 [8], P('lay'), may hold values from 0.1 to 1
- layer_temp: float32 [8], P('lay'), may hold values from 200 to 300
- column_index: int32 [32, 8], replicated, may hold values from 0 to 63
- column_table: float32 [3, 64], replicated, may hold values from 0.03 to 0.3
- noise_var: float32 [65536], P(('spec', 'line')), may hold values from 1e-05 to 0.0004
Outputs:
- transmit: float32 [32, 65536], P(None, ('spec', 'line'))
- normals: float32 [32, 24, 24], P(None, 'lay')
Inputs may be any that keep to these rules, and one draw needn't show every extreme that they name: `cutoff`: blocks are numbered in order, 32 to each index d of spec+line; tile t belongs to index t // 4. A block's entries that are not -1 come first, are distinct, and name tiles of indices d - 1, d and d + 1; every block has at least one such entry, some have 4.
All inputs are finite; a program needn't handle non-finite values.
Results may differ from a plain program's by a relative error of at most 0.0003.
Values sent between devices are 32-bit elements; how exact they have to be, the bound alone decides.
No kernel may reach another device: no remote copies, remote signals or barrier semaphores. Data moves between devices by JAX's collectives and lax.ppermute only.
A program may use at most 192 MiB of HBM per device.

v0:
```python
import math

import jax
import jax.numpy as jnp
from jax import lax
from jax.sharding import PartitionSpec as P

TILE = 256


HIGH = lax.Precision.HIGHEST
LN_TWO = math.log(2.0)
C_TWO = 1.4388


def passed_along(value, axis, by):
    peers = lax.axis_size(axis)
    pairs = [(i, i + by) for i in range(peers) if 0 <= i + by < peers]
    return lax.ppermute(value, axis, pairs)


def profile_widths(lorentz, gauss):
    full_width = (
        gauss**5
        + 2.69269 * gauss**4 * lorentz
        + 2.42843 * gauss**3 * lorentz**2
        + 4.47163 * gauss**2 * lorentz**3
        + 0.07842 * gauss * lorentz**4
        + lorentz**5
    ) ** 0.2
    width_ratio = lorentz / full_width
    mixing = 1.36603 * width_ratio - 0.47719 * width_ratio**2 + 0.11116 * width_ratio**3
    return (full_width, mixing)


def profile_shape(distance, full_width, mixing):
    half_width = 0.5 * full_width
    lorentz_part = half_width / math.pi / (distance * distance + half_width * half_width)
    gauss_part = (
        math.sqrt(4.0 * LN_TWO / math.pi)
        / full_width
        * jnp.exp(-4.0 * LN_TWO * distance * distance / (full_width * full_width))
    )
    return mixing * lorentz_part + (1.0 - mixing) * gauss_part


def block_terms(offset, strength, energy, lwidth, dwidth, species, near_list, pressure, temper):
    lines_here = offset.shape[0]
    valid_count = jnp.maximum(jnp.sum((near_list >= 0).astype(jnp.int32)), 1)
    slot_index = jnp.arange(lines_here, dtype=jnp.int32) % valid_count
    home_tile = near_list[slot_index]
    temp_ratio = 296.0 / temper
    lorentz = lwidth[None, :] * (pressure * temp_ratio**0.75)[:, None]
    gauss = dwidth[None, :] * jnp.sqrt(temper / 296.0)[:, None]
    layer_strength = strength[None, :] * jnp.exp(
        -C_TWO * energy[None, :] * (1.0 / temper - 1.0 / 296.0)[:, None]
    )
    species_rows = (species[None, :] == jnp.arange(3, dtype=jnp.float32)[:, None]).astype(
        jnp.float32
    )
    weights = layer_strength[:, None, :] * species_rows[None, :, :]
    tile_steps = (near_list[:, None] - home_tile[None, :]) * TILE
    grid_steps = tile_steps[:, :, None] + jnp.arange(TILE, dtype=jnp.int32)[None, None, :]
    distance = grid_steps.astype(jnp.float32) - offset[None, :, None]
    full_width, mixing = profile_widths(lorentz, gauss)
    profile = profile_shape(
        distance[:, None], full_width[None, :, :, None], mixing[None, :, :, None]
    )
    tile_terms = jnp.einsum("lsk,jlkp->jlsp", weights, profile, precision=HIGH)
    return tile_terms.reshape(near_list.shape[0], -1)


def body(
    line_offset,
    line_strength,
    lower_energy,
    lorentz_width,
    doppler_width,
    line_species,
    cutoff,
    layer_pressure,
    layer_temp,
    column_index,
    column_table,
    noise_var,
):
    tiles_dev = noise_var.shape[0] // TILE
    groups = lax.axis_size(("spec", "line"))
    total_tiles = tiles_dev * groups
    position = lax.axis_index(("spec", "line"))
    near_count = cutoff.shape[1]
    species_real = line_species.astype(jnp.float32)
    block_total = cutoff.shape[0]

    def by_block(values):
        return values.reshape(block_total, -1)

    mapped = jax.vmap(block_terms, in_axes=(0, 0, 0, 0, 0, 0, 0, None, None))
    result = mapped(
        by_block(line_offset),
        by_block(line_strength),
        by_block(lower_energy),
        by_block(lorentz_width),
        by_block(doppler_width),
        by_block(species_real),
        cutoff,
        layer_pressure,
        layer_temp,
    )
    tile_terms = result.reshape(block_total * near_count, -1)
    window_base = (position - 1) * tiles_dev
    wanted = window_base + jnp.arange(3 * tiles_dev, dtype=jnp.int32)
    selector = (cutoff.reshape(-1)[None, :] == wanted[:, None]).astype(jnp.float32)
    window = jnp.dot(selector, tile_terms, precision=HIGH)
    lower_part = window[:tiles_dev]
    middle = window[tiles_dev : 2 * tiles_dev]
    upper_part = window[2 * tiles_dev :]
    from_above = passed_along(lower_part, ("spec", "line"), -1)
    from_below = passed_along(upper_part, ("spec", "line"), 1)
    owned_tiles = middle + from_above + from_below
    row_count = owned_tiles.shape[1] // TILE
    cross_own = (
        owned_tiles.reshape(tiles_dev, row_count, TILE)
        .transpose(1, 0, 2)
        .reshape(row_count, tiles_dev * TILE)
    )
    table_size = column_table.shape[1]
    soundings = column_index.shape[0]
    chosen = (
        column_index[:, :, None] == jnp.arange(table_size, dtype=jnp.int32)[None, None, :]
    ).astype(jnp.float32)
    amounts = jnp.einsum("slc,pc->slp", chosen, column_table, precision=HIGH).reshape(soundings, -1)
    layer_slot = lax.axis_index("lay")
    own_amounts = lax.dynamic_slice_in_dim(amounts, layer_slot * row_count, row_count, 1)
    spectral = total_tiles * TILE
    local_depth = jnp.dot(own_amounts, cross_own, precision=HIGH)
    optical_depth = lax.psum(local_depth, "lay")
    transmit = jnp.exp(-optical_depth)
    weight = transmit * transmit / noise_var[None, :] / spectral
    scaled = cross_own[None, :, :] * weight[:, None, :] * own_amounts[:, :, None]
    gram_block = jnp.einsum(
        "sav,bv->sab", scaled, lax.all_gather(cross_own, "lay", axis=0, tiled=True), precision=HIGH
    )
    partial_normals = gram_block * amounts[:, None, :]
    normals = lax.psum(partial_normals, ("spec", "line"))
    return (transmit, normals)


def solution(mesh):
    in_specs = (
        P(("spec", "line")),
        P(("spec", "line")),
        P(("spec", "line")),
        P(("spec", "line")),
        P(("spec", "line")),
        P(("spec", "line")),
        P(("spec", "line"), None),
        P("lay"),
        P("lay"),
        P(),
        P(),
        P(("spec", "line")),
    )
    out_specs = (P(None, ("spec", "line")), P(None, "lay", None))
    return jax.shard_map(body, mesh=mesh, in_specs=in_specs, out_specs=out_specs, check_vma=False)
```

profile of v0, /device:TPU:4, one launch (start us, length us, event | category | flops | bytes accessed | tf_op | source)
XLA Modules:
  0.0 461.4 jit_solution(8648406682532753813)
XLA Ops:
  7.3 0.8 copy.22
  8.0 0.7 convert_reduce_fusion
  8.7 0.7 divide_add_fusion
  9.4 0.9 power_multiply_fusion.2
  10.5 0.3 fusion.49
  10.8 29.9 %gather_fusion = s32[4096]{0:T(1024)S(1)} fusion(s32[32,4]{0,1:T(4,128)} %param.18, s32[4096]{0:T(1024)S(1)} %fusion.49), kind=kCustom, calls=%fused_computation | custom fusion | bytes 65536 | tf_op jit(solution)/shard_map/vmap()/gather | solution.py:51
  40.7 0.1 eq.58
  40.8 0.1 subtract_multiply_fusion
  41.0 3.9 fusion.11
  44.9 0.1 exponential_multiply_fusion
  45.0 36.0 %fusion.14 = f32[32,4,2,3,256]{4,3,1,2,0:T(4,128)S(1)} fusion(f32[32,2,128]{2,1,0:T(2,128)S(1)} %copy.29, f32[32,4,128,256]{3,2,1,0:T(8,128)S(1)} %get-tuple-element.9, f32[32,2,128]{2,1,0:T(2,128)S(1)} %copy.28, f32[32,2,128]{2,1,0:T(2,128)S(1)} %copy.27, f32[32,2,128]{2,1,0:T(2,128)S(1)} %copy.26, f32[32,4,128,256]{3,2,1,0:T(8,128)S(1)} %get-tuple-element.8, ...), kind=kOutput, calls=%fused_computation.17 | convolution fusion | flops 360734720 | bytes 34619392 | tf_op jit(solution)/shard_map/vmap(lsk,jlkp->jlsp)/dot_general | solution.py:69
  81.0 0.2 copy.30
  81.2 0.5 reshape.196
  81.8 0.4 fusion.53
  82.2 1.3 collective-permute-start
  83.5 4.5 collective-permute-start.1
  88.0 0.4 fusion.24
  88.5 1.0 collective-permute-done.1
  89.5 1.0 fusion.60
  90.6 6.9 %all-gather = f32[4,6,1024]{2,1,0:T(8,128)S(1)} all-gather(f32[1,6,1024]{2,1,0:T(8,128)S(1)} %bitcast.33), channel_id=1, replica_groups=mesh['spec'=16,'line'=4,'lay'=4] {'lay'}, dimensions={0}, use_global_device_ids=true | all-gather | bytes 122880 | tf_op jit(solution)/shard_map/all_gather | solution.py:142
  97.5 44.0 %all-reduce.2.cloned.1.call-done = f32[32,1024]{1,0:T(8,128)} async-done(((f32[32,1024]{1,0:T(8,128)}), f32[32,1024]{1,0:T(8,128)}) %all-reduce.2.cloned.1.call-update) | async-done | bytes 131088 | tf_op jit(solution)/shard_map/psum | solution.py:137
  141.6 1.6 divide_multiply_fusion
  143.2 1.7 convolution_multiply_fusion
  144.9 309.7 %psum.15 = f32[32,6,24]{0,2,1:T(8,128)} all-reduce(f32[32,6,24]{0,2,1:T(8,128)S(1)} %convolution_multiply_fusion), channel_id=1, replica_groups=mesh['spec'=16,'line'=4,'lay'=4] {'spec','line'}, use_global_device_ids=true, to_apply=%region_2.3 | all-reduce | flops 4608 | bytes 36864 | tf_op jit(solution)/shard_map/psum | solution.py:145
  (34 shorter events, 0.4 us)
Async XLA Ops:
  7.2 80.9 %copy-start = (f32[3,64]{1,0:T(4,128)S(1)}, f32[3,64]{1,0:T(4,128)}, u32[]{:S(2)}) copy-start(f32[3,64]{1,0:T(4,128)} %param.22) | copy-start | bytes 2308
  7.2 33.7 %copy-start.2 = (f32[4096]{0:T(1024)S(1)}, f32[4096]{0:T(1024)}, u32[]{:S(2)}) copy-start(f32[4096]{0:T(1024)} %param.14) | copy-start | bytes 49156
  7.2 33.7 %copy-start.3 = (s32[4096]{0:T(1024)S(1)}, s32[4096]{0:T(1024)}, u32[]{:S(2)}) copy-start(s32[4096]{0:T(1024)} %param.17) | copy-start | bytes 49156
  7.2 33.7 %copy-start.1 = (f32[4096]{0:T(1024)S(1)}, f32[4096]{0:T(1024)}, u32[]{:S(2)}) copy-start(f32[4096]{0:T(1024)} %param.12) | copy-start | bytes 49156
  7.2 134.3 %all-reduce.2.cloned.1.call-start = ((), (), s32[]{:S(2)}) async-start(), calls=%async_computation | async-start | bytes 262144 | tf_op jit(solution)/shard_map/psum | solution.py:137
  41.0 3.9 copy-start.4
  45.0 43.1 %copy-start.6 = (s32[32,8]{0,1:T(8,128)S(1)}, s32[32,8]{0,1:T(8,128)}, u32[]{:S(2)}) copy-start(s32[32,8]{0,1:T(8,128)} %param.21) | copy-start | bytes 3076
  45.0 96.6 %copy-start.5 = (f32[1024]{0:T(1024)S(1)}, f32[1024]{0:T(1024)}, u32[]{:S(2)}) copy-start(f32[1024]{0:T(1024)} %param.23) | copy-start | bytes 12292
  82.2 6.4 %collective-permute-start = (f32[4,1536]{1,0:T(4,128)S(1)}, f32[4,1536]{1,0:T(4,128)S(1)}, u32[]{:S(2)}, u32[]{:S(2)}) collective-permute-start(f32[4,1536]{1,0:T(4,128)S(1)} %get-tuple-element.6), channel_id=1, source_target_pairs={{4,0},{8,4},{12,8},{16,12},{20,16},{24,20},{28,24},{32,28},{36,32}... | collective-permute-start | bytes 73736 | tf_op jit(solution)/shard_map/ppermute | solution.py:19
  83.5 6.1 %collective-permute-start.1 = (f32[4,1536]{1,0:T(4,128)S(1)}, f32[4,1536]{1,0:T(4,128)S(1)}, u32[]{:S(2)}, u32[]{:S(2)}) collective-permute-start(f32[4,1536]{1,0:T(4,128)S(1)} %get-tuple-element.7), channel_id=1, source_target_pairs={{0,4},{4,8},{8,12},{12,16},{16,20},{20,24},{24,28},{28,32},{32,36}... | collective-permute-start | bytes 73736 | tf_op jit(solution)/shard_map/ppermute | solution.py:19
Sparse Core Ops, SparseCore 0:
  90.7 50.8 all-reduce.1
where the time goes:
time: 462 us; the launch traced here: 461 us
  blocking collectives  317 us (69%)
  waiting for transfers between devices  45 us (10%)
  matrix products  39.5 us (9%)
  local copies, waits for them, and re-layouts  31.8 us (7%)
  between operations  14.3 us (3%)
  other arithmetic  8.27 us (2%)
  starting transfers between devices  5.88 us (1%)
    psum x1, blocking collectives, body(): normals = lax.psum(partial_normals, ('spec', 'line'))  310 us
    psum x1, waiting for transfers between devices, body(): optical_depth = lax.psum(local_depth, 'lay')  44 us
    dot_general x1, matrix products, block_terms(): tile_terms = jnp.einsum('lsk,jlkp->jlsp', weights, profile, precision=HIGH)  36 us
    gather x1, local copies, waits for them, and re-layouts, block_terms(): home_tile = near_list[slot_index]  29.9 us
  transfers between devices with their start and end apart: 3, of which 2 were waited for; matrix products, arithmetic and copies ran while one was open for 0% of the time, Pallas kernels for 0%

commit v1 on v0

--- a/solution.py
+++ b/solution.py
@@ -17,6 +17,17 @@
     peers = lax.axis_size(axis)
     pairs = [(i, i + by) for i in range(peers) if 0 <= i + by < peers]
     return lax.ppermute(value, axis, pairs)
+
+
+def summed_over(value, axis, total, size, stride):
+    members = [
+        [base + stride * k for k in range(size)]
+        for base in range(total)
+        if (base // stride) % size == 0
+    ]
+    copies = jnp.broadcast_to(value[None], (size,) + value.shape)
+    landed = lax.all_to_all(copies, axis, 0, 0, axis_index_groups=members, tiled=True)
+    return jnp.sum(landed, axis=0)
 
 
 def profile_widths(lorentz, gauss):
@@ -48,7 +59,14 @@
     lines_here = offset.shape[0]
     valid_count = jnp.maximum(jnp.sum((near_list >= 0).astype(jnp.int32)), 1)
     slot_index = jnp.arange(lines_here, dtype=jnp.int32) % valid_count
-    home_tile = near_list[slot_index]
+    home_tile = jnp.sum(
+        jnp.where(
+            slot_index[None, :] == jnp.arange(near_list.shape[0], dtype=jnp.int32)[:, None],
+            near_list[:, None],
+            0,
+        ),
+        axis=0,
+    )
     temp_ratio = 296.0 / temper
     lorentz = lwidth[None, :] * (pressure * temp_ratio**0.75)[:, None]
     gauss = dwidth[None, :] * jnp.sqrt(temper / 296.0)[:, None]
@@ -133,16 +151,22 @@
     layer_slot = lax.axis_index("lay")
     own_amounts = lax.dynamic_slice_in_dim(amounts, layer_slot * row_count, row_count, 1)
     spectral = total_tiles * TILE
-    local_depth = jnp.dot(own_amounts, cross_own, precision=HIGH)
-    optical_depth = lax.psum(local_depth, "lay")
+    cross_all = lax.all_gather(cross_own, "lay", axis=0, tiled=True)
+    optical_depth = jnp.dot(amounts, cross_all, precision=HIGH)
     transmit = jnp.exp(-optical_depth)
     weight = transmit * transmit / noise_var[None, :] / spectral
     scaled = cross_own[None, :, :] * weight[:, None, :] * own_amounts[:, :, None]
     gram_block = jnp.einsum(
-        "sav,bv->sab", scaled, lax.all_gather(cross_own, "lay", axis=0, tiled=True), precision=HIGH
+        "sav,bv->sab", scaled, cross_all, precision=HIGH
     )
     partial_normals = gram_block * amounts[:, None, :]
-    normals = lax.psum(partial_normals, ("spec", "line"))
+    flat = partial_normals.reshape(-1, 128)
+    stride = 1
+    while stride < groups:
+        size = min(8, groups // stride)
+        flat = summed_over(flat, ("spec", "line"), groups, size, stride)
+        stride *= size
+    normals = flat.reshape(partial_normals.shape)
     return (transmit, normals)
 
 

time: 462 us -> 101 us (0.22)
  blocking collectives: 317 us -> 41.7 us
  waiting for transfers between devices: 45 us -> 1 us
  local copies, waits for them, and re-layouts: 31.8 us -> 2.98 us
  between operations: 14.3 us -> 0.94 us
    psum x1 -> x0, blocking collectives: 310 us -> none  [body(): normals = lax.psum(partial_normals, ('spec', 'line'))]
    psum x1 -> x0, waiting for transfers between devices: 44 us -> none  [body(): optical_depth = lax.psum(local_depth, 'lay')]
    all_to_all x0 -> x2, blocking collectives: none -> 34.8 us  [summed_over(): lax.all_to_all(copies, axis, 0, 0, axis_index_groups=members, tiled=True)]
    gather x1 -> x0, local copies, waits for them, and re-layouts: 29.9 us -> none  [block_terms(): home_tile = near_list[slot_index]]
  transfers between devices with their start and end apart: 3 -> 2, of which waited for: 2 -> 1; matrix products, arithmetic and copies ran while one was open for 0% -> 0% of each run, Pallas kernels for 0% -> 0%
where the time goes in v1:
time: 101 us
  blocking collectives  41.7 us (41%)
  matrix products  39.3 us (39%)
  other arithmetic  8.97 us (9%)
  starting transfers between devices  5.84 us (6%)
  local copies, waits for them, and re-layouts  2.98 us (3%)
    dot_general x1, matrix products, block_terms(): tile_terms = jnp.einsum('lsk,jlkp->jlsp', weights, profile, precision=HIGH)  35.8 us
    all_to_all x2, blocking collectives, summed_over(): lax.all_to_all(copies, axis, 0, 0, axis_index_groups=members, tiled=True)  34.8 us
    all_gather x1, blocking collectives, body(): cross_all = lax.all_gather(cross_own, 'lay', axis=0, tiled=True)  6.93 us
    ppermute x2, starting transfers between devices, passed_along(): return lax.ppermute(value, axis, pairs)  5.84 us
    mul x1, other arithmetic, profile_shape(): distance * distance + half_width * half_width  4.6 us
  transfers between devices with their start and end apart: 2, of which 1 were waited for; matrix products, arithmetic and copies ran while one was open for 0% of the time, Pallas kernels for 0%

profile of v1, /device:TPU:4, one launch (start us, length us, event | category | flops | bytes accessed | tf_op | source)
XLA Modules:
  0.0 100.7 jit_solution(15162422622803094955)
XLA Ops:
  0.6 0.8 copy.38
  1.4 0.7 convert_reduce_fusion
  2.1 0.7 divide_add_fusion
  2.8 0.9 power_multiply_fusion.2
  3.9 0.3 add_select_fusion
  4.3 0.1 select_reduce_fusion
  4.5 0.7 multiply_bitcast_fusion
  5.2 0.7 convert_bitcast_fusion
  6.0 4.6 %fusion.11 = (f32[32,4,128,256]{3,2,1,0:T(8,128)S(1)}, f32[32,4,128,256]{3,2,1,0:T(8,128)S(1)}) fusion(f32[32,128]{1,0:T(8,128)} %bitcast.31, s32[32,4,128]{2,1,0:T(4,128)S(1)} %subtract_multiply_fusion), kind=kLoop, calls=%fused_computation.13 | loop fusion | flops 25165824 | bytes 33636352 | tf_op jit(solution)/shard_map/vmap()/mul | solution.py:49
  10.7 35.8 %fusion.14 = f32[32,4,2,3,256]{4,3,1,2,0:T(4,128)S(1)} fusion(f32[32,2,128]{2,1,0:T(2,128)S(1)} %copy.45, f32[32,4,128,256]{3,2,1,0:T(8,128)S(1)} %get-tuple-element.17, f32[32,2,128]{2,1,0:T(2,128)S(1)} %copy.44, f32[32,2,128]{2,1,0:T(2,128)S(1)} %copy.43, f32[32,2,128]{2,1,0:T(2,128)S(1)} %copy.42, f32[32,4,128,256]{3,2,1,0:T(8,128)S(1)} %get-tuple-element.16, ...), kind=kOutput, calls=%fused_computation.16 | convolution fusion | flops 360734720 | bytes 34619392 | tf_op jit(solution)/shard_map/vmap(lsk,jlkp->jlsp)/dot_general | solution.py:87
  46.5 0.2 copy.46
  46.8 0.5 reshape.159
  47.3 0.4 fusion.50
  47.7 1.3 %collective-permute-start = (f32[4,1536]{1,0:T(4,128)S(1)}, f32[4,1536]{1,0:T(4,128)S(1)}, u32[]{:S(2)}, u32[]{:S(2)}) collective-permute-start(f32[4,1536]{1,0:T(4,128)S(1)} %get-tuple-element.14), channel_id=1, source_target_pairs={{4,0},{8,4},{12,8},{16,12},{20,16},{24,20},{28,24},{32,28},{36,32}... | collective-permute-start | bytes 73736 | tf_op jit(solution)/shard_map/ppermute | solution.py:19
  49.0 4.5 %collective-permute-start.1 = (f32[4,1536]{1,0:T(4,128)S(1)}, f32[4,1536]{1,0:T(4,128)S(1)}, u32[]{:S(2)}, u32[]{:S(2)}) collective-permute-start(f32[4,1536]{1,0:T(4,128)S(1)} %get-tuple-element.15), channel_id=1, source_target_pairs={{0,4},{4,8},{8,12},{12,16},{16,20},{20,24},{24,28},{28,32},{32,36}... | collective-permute-start | bytes 73736 | tf_op jit(solution)/shard_map/ppermute | solution.py:19
  53.6 0.4 fusion.25
  54.1 1.0 collective-permute-done.1
  55.1 6.9 %all-gather = f32[4,6,1024]{2,1,0:T(8,128)S(1)} all-gather(f32[1,6,1024]{2,1,0:T(8,128)S(1)} %bitcast.29), channel_id=1, replica_groups=mesh['spec'=16,'line'=4,'lay'=4] {'lay'}, dimensions={0}, use_global_device_ids=true | all-gather | bytes 122880 | tf_op jit(solution)/shard_map/all_gather | solution.py:154
  62.1 1.0 divide_multiply_fusion
  63.1 1.7 %convolution_multiply_fusion = f32[32,6,24]{0,2,1:T(8,128)S(1)} fusion(f32[24,1024,1]{1,0,2:T(8,128)S(1)} %reshape.168, f32[32,6]{0,1:T(8,128)S(1)} %constant_dynamic-slice_fusion, f32[32,1024]{1,0:T(8,128)S(1)} %get-tuple-element.27, f32[6,1024]{1,0:T(8,128)S(1)} %bitcast.30, f32[32,24]{0,1:T(8,128)S(1)} %reshape.158), kind=kOutput, calls=%fused_computation.19 | convolution fusion | flops 57020928 | bytes 276224 | tf_op jit(solution)/shard_map/sav,bv->sab/dot_general | solution.py:159
  64.8 0.1 copy.47
  65.0 14.7 %all_to_all.10 = f32[8,36,128]{2,1,0:T(8,128)S(1)} all-to-all(f32[8,36,128]{2,1,0:T(8,128)S(1)} %broadcast_in_dim.29), channel_id=1, replica_groups={{0,4,8,12,16,20,24,28},{32,36,40,44,48,52,56,60},{64,68,72,76,80,84,88,..., dimensions={0} | all-to-all | bytes 294912 | tf_op jit(solution)/shard_map/all_to_all | solution.py:29
  79.8 20.1 %all_to_all.11 = f32[8,36,128]{2,1,0:T(8,128)S(1)} all-to-all(f32[8,36,128]{2,1,0:T(8,128)S(1)} %broadcast_in_dim.30), channel_id=1, replica_groups={{0,32,64,96,128,160,192,224},{4,36,68,100,132,164,196,228},{8,40,72,104..., dimensions={0} | all-to-all | bytes 294912 | tf_op jit(solution)/shard_map/all_to_all | solution.py:29
  100.0 0.7 copy.50
  (34 shorter events, 0.9 us)
Async XLA Ops:
  0.6 52.9 %copy-start = (f32[3,64]{1,0:T(4,128)S(1)}, f32[3,64]{1,0:T(4,128)}, u32[]{:S(2)}) copy-start(f32[3,64]{1,0:T(4,128)} %param.22) | copy-start | bytes 2308
  6.0 4.6 %copy-start.1 = (f32[4096]{0:T(1024)S(1)}, f32[4096]{0:T(1024)}, u32[]{:S(2)}) copy-start(f32[4096]{0:T(1024)} %param.13) | copy-start | bytes 49156
  10.7 42.9 %copy-start.2 = (s32[32,8]{0,1:T(8,128)S(1)}, s32[32,8]{0,1:T(8,128)}, u32[]{:S(2)}) copy-start(s32[32,8]{0,1:T(8,128)} %param.21) | copy-start | bytes 3076
  10.7 51.4 %copy-start.3 = (f32[1024]{0:T(1024)S(1)}, f32[1024]{0:T(1024)}, u32[]{:S(2)}) copy-start(f32[1024]{0:T(1024)} %param.23) | copy-start | bytes 12292
  47.7 6.4 %collective-permute-start = (f32[4,1536]{1,0:T(4,128)S(1)}, f32[4,1536]{1,0:T(4,128)S(1)}, u32[]{:S(2)}, u32[]{:S(2)}) collective-permute-start(f32[4,1536]{1,0:T(4,128)S(1)} %get-tuple-element.14), channel_id=1, source_target_pairs={{4,0},{8,4},{12,8},{16,12},{20,16},{24,20},{28,24},{32,28},{36,32}... | collective-permute-start | bytes 73736 | tf_op jit(solution)/shard_map/ppermute | solution.py:19
  49.0 6.1 %collective-permute-start.1 = (f32[4,1536]{1,0:T(4,128)S(1)}, f32[4,1536]{1,0:T(4,128)S(1)}, u32[]{:S(2)}, u32[]{:S(2)}) collective-permute-start(f32[4,1536]{1,0:T(4,128)S(1)} %get-tuple-element.15), channel_id=1, source_target_pairs={{0,4},{4,8},{8,12},{12,16},{16,20},{20,24},{24,28},{28,32},{32,36}... | collective-permute-start | bytes 73736 | tf_op jit(solution)/shard_map/ppermute | solution.py:19

commit v2 on v1

v2 whole, which is shorter than its diff:
```python
import functools
import math

import jax
import jax.numpy as jnp
from jax import lax
from jax.experimental import pallas as pl
from jax.experimental.pallas import tpu as pltpu
from jax.sharding import PartitionSpec as P

TILE = 256
LBLK = 128
NEAR = 4
SPECIES = 3
OWN_TILES = 4
GROUP = ("spec", "line")

HIGH = lax.Precision.HIGHEST
LN_TWO = math.log(2.0)
C_TWO = 1.4388
VMEM_BYTES = 40 * 1024 * 1024


def passed_along(value, by):
    peers = lax.axis_size(GROUP)
    pairs = [(i, i + by) for i in range(peers) if 0 <= i + by < peers]
    return lax.ppermute(value, GROUP, pairs)


def summed_over(copies, total, size, stride):
    members = [
        [base + stride * k for k in range(size)]
        for base in range(total)
        if (base // stride) % size == 0
    ]
    landed = lax.all_to_all(copies, GROUP, 0, 0, axis_index_groups=members, tiled=True)
    return jnp.sum(landed, axis=0)


def line_tables(near, temper_ref, press_ref, lines, home_ref, rate_ref, mix_ref, amp_ref):
    offset, strength, energy, lwidth, dwidth = lines
    shape = strength.shape
    count = jnp.sum((near >= 0).astype(jnp.int32), axis=1, keepdims=True)
    lane = lax.broadcasted_iota(jnp.int32, shape, 1)
    entry = jnp.where(
        count == 3,
        lax.rem(lane, 3),
        jnp.where(count == 4, lane & 3, jnp.where(count == 2, lane & 1, 0)),
    )
    home = near[:, NEAR - 1 : NEAR]
    for j in range(NEAR - 2, -1, -1):
        home = jnp.where(entry == j, near[:, j : j + 1], home)
    home_ref[...] = (home * TILE).astype(jnp.float32)
    for layer in range(2):
        temper = jnp.full(shape, temper_ref[layer], jnp.float32)
        ratio = 296.0 / temper
        lor = lwidth * (press_ref[layer] * jnp.exp(0.75 * jnp.log(ratio)))
        gau = dwidth * jnp.sqrt(temper / 296.0)
        line = strength * jnp.exp(-C_TWO * energy * (1.0 / temper - 1.0 / 296.0))
        g2 = gau * gau
        g4 = g2 * g2
        l2 = lor * lor
        l4 = l2 * l2
        total = (
            g4 * gau
            + 2.69269 * g4 * lor
            + 2.42843 * g2 * gau * l2
            + 4.47163 * g2 * lor * l2
            + 0.07842 * gau * l4
            + l4 * lor
        )
        width = jnp.exp(0.2 * jnp.log(total))
        inverse = 1.0 / width
        part = lor * inverse
        eta = part * (1.36603 + part * (-0.47719 + part * 0.11116))
        peak = eta * (2.0 / math.pi)
        rate_ref[layer] = -4.0 * inverse * inverse
        mix_ref[layer] = (1.0 - eta) * math.sqrt(4.0 * LN_TWO / math.pi) / peak
        amp_ref[layer] = line * peak * inverse


def pairs_kernel(
    outward,
    place_ref,
    near_ref,
    press_ref,
    temper_ref,
    near_hbm,
    offset_hbm,
    strength_hbm,
    energy_hbm,
    lwidth_hbm,
    dwidth_hbm,
    species_hbm,
    *rest,
):
    if outward:
        outs, scratch = rest[:2], rest[2:]
    else:
        index_ref, table_ref = rest[:2]
        outs, scratch = rest[2:5], rest[5:]
    (
        near_v,
        offset_v,
        strength_v,
        energy_v,
        lwidth_v,
        dwidth_v,
        species_v,
        sems,
        home_ref,
        rate_ref,
        mix_ref,
        amp_ref,
        acc_ref,
        list_ref,
        buf_a,
        buf_b,
    ) = scratch
    hbm = (near_hbm, offset_hbm, strength_hbm, energy_hbm, lwidth_hbm, dwidth_hbm, species_hbm)
    vmem = (near_v, offset_v, strength_v, energy_v, lwidth_v, dwidth_v, species_v)
    copies = [pltpu.make_async_copy(s, d, sems.at[i]) for i, (s, d) in enumerate(zip(hbm, vmem))]
    for copy in copies:
        copy.start()

    slots = acc_ref.shape[0] - 1
    blocks = near_v.shape[0]
    base = (place_ref[0] - 1) * OWN_TILES + (0 if outward else OWN_TILES)
    trash = slots * blocks
    list_ref[0] = jnp.int32(trash)
    found = jnp.int32(1)
    for b in range(blocks):
        for j in range(NEAR):
            tile = near_ref[b * NEAR + j]
            slot = tile - base
            valid = tile >= 0
            if outward:
                above = slot >= 2 * OWN_TILES
                valid &= (slot < OWN_TILES) | above
                slot = jnp.where(above, slot - OWN_TILES, slot)
            else:
                valid &= (slot >= 0) & (slot < OWN_TILES)
            list_ref[found] = slot * blocks + b
            found = found + valid.astype(jnp.int32)
    list_ref[found] = jnp.int32(trash)
    acc_ref[...] = jnp.zeros_like(acc_ref)

    for copy in copies:
        copy.wait()
    line_tables(
        near_v[...],
        temper_ref,
        press_ref,
        (offset_v[...], strength_v[...], energy_v[...], lwidth_v[...], dwidth_v[...]),
        home_ref,
        rate_ref,
        mix_ref,
        amp_ref,
    )

    rows = 16
    row = lax.broadcasted_iota(jnp.int32, (rows, LBLK), 0)
    part = row // SPECIES
    kind = row - part * SPECIES
    point = lax.broadcasted_iota(jnp.int32, (16, LBLK), 0).astype(jnp.float32)

    def decode(i):
        code = list_ref[i]
        return lax.div(code, blocks), lax.rem(code, blocks)

    def evaluate(i, buf):
        slot, b = decode(i)
        tile = slot + base
        if outward:
            tile = jnp.where(slot >= OWN_TILES, tile + OWN_TILES, tile)
        shift = ((tile * TILE).astype(jnp.float32) - home_ref[pl.ds(b, 1), :]) - offset_v[
            pl.ds(b, 1), :
        ]
        rate = [rate_ref[layer, pl.ds(b, 1), :] for layer in range(2)]
        mix = [mix_ref[layer, pl.ds(b, 1), :] for layer in range(2)]
        for k in range(0, TILE, 16):
            x = point + (shift + float(k))
            square = x * x
            for layer in range(2):
                q = square * rate[layer]
                value = 1.0 / (1.0 - q) + mix[layer] * jnp.exp2(q)
                high = value.astype(jnp.bfloat16)
                buf[layer, k : k + 16, :LBLK] = high
                buf[layer, k : k + 16, LBLK:] = (value - high.astype(jnp.float32)).astype(
                    jnp.bfloat16
                )

    def reduce(i, buf):
        slot, b = decode(i)
        same = kind == species_v[pl.ds(b, 1), :]
        for layer in range(2):
            amp = jnp.broadcast_to(amp_ref[layer, pl.ds(b, 1), :], (rows, LBLK))
            one = amp.astype(jnp.bfloat16).astype(jnp.float32)
            left = amp - one
            two = left.astype(jnp.bfloat16).astype(jnp.float32)
            split = jnp.where(
                part == 0, one, jnp.where(part == 1, two, jnp.where(part == 2, left - two, 0.0))
            )
            weights = jnp.where(same, split, 0.0).astype(jnp.bfloat16)
            weights = jnp.concatenate([weights, weights], axis=1)
            acc_ref[slot, layer] += lax.dot_general(
                weights,
                buf[layer],
                (((1,), (1,)), ((), ())),
                preferred_element_type=jnp.float32,
            )

    def step(i, carry):
        evaluate(2 * i + 1, buf_a)
        reduce(2 * i, buf_b)
        evaluate(2 * i + 2, buf_b)
        reduce(2 * i + 1, buf_a)
        return carry

    turns = lax.div(found, 2)
    lax.fori_loop(0, turns, step, 0)
    reduce(2 * turns, buf_b)

    for slot in range(slots):
        out = outs[slot // OWN_TILES]
        at = (slot % OWN_TILES) * TILE
        for layer in range(2):
            sums = acc_ref[slot, layer]
            out[SPECIES * layer : SPECIES * (layer + 1), at : at + TILE] = (
                sums[:SPECIES] + sums[SPECIES : 2 * SPECIES] + sums[2 * SPECIES : 3 * SPECIES]
            )

    if not outward:
        amount_tables(place_ref[1], index_ref, table_ref, outs[1], outs[2])


def amount_tables(lay, index_ref, table_ref, amounts_ref, factor_ref):
    sounds, layers = index_ref.shape
    entries = table_ref.shape[1]
    columns = layers * SPECIES
    lane = lax.broadcasted_iota(jnp.int32, (sounds, columns), 1)
    entry = lax.broadcasted_iota(jnp.int32, (sounds, entries), 1)
    amounts = jnp.zeros((sounds, columns), jnp.float32)
    for layer in range(layers):
        hit = entry == index_ref[:, layer : layer + 1]
        for kind in range(SPECIES):
            column = jnp.sum(
                jnp.where(hit, table_ref[kind : kind + 1, :], 0.0), axis=1, keepdims=True
            )
            amounts = jnp.where(lane == SPECIES * layer + kind, column, amounts)
    amounts_ref[...] = amounts
    own = factor_ref.shape[0]
    for a in range(own):
        column = jnp.sum(
            jnp.where(lane == own * lay + a, amounts, 0.0), axis=1, keepdims=True
        )
        factor_ref[a] = column * amounts


def pair_sums(outward, place, near, press, temper, lines, index=None, table=None):
    blocks = near.shape[0]
    row_count = 2 * SPECIES
    width = OWN_TILES * TILE
    smem = pl.BlockSpec(memory_space=pltpu.SMEM)
    vmem = pl.BlockSpec(memory_space=pltpu.VMEM)
    hbm = pl.BlockSpec(memory_space=pl.ANY)
    block_shape = (blocks, LBLK)
    f32 = functools.partial(pltpu.VMEM, dtype=jnp.float32)
    slots = (2 if outward else 1) * OWN_TILES
    sums = jax.ShapeDtypeStruct((row_count, width), jnp.float32)
    in_specs = [smem] * 4 + [hbm] * 7
    args = [place, near.reshape(-1), press, temper, near] + [v.reshape(block_shape) for v in lines]
    if outward:
        out_shape = (sums, sums)
    else:
        sounds, layers = index.shape
        columns = layers * SPECIES
        out_shape = (
            sums,
            jax.ShapeDtypeStruct((sounds, columns), jnp.float32),
            jax.ShapeDtypeStruct((row_count, sounds, columns), jnp.float32),
        )
        in_specs += [vmem] * 2
        args += [index, table]
    return pl.pallas_call(
        functools.partial(pairs_kernel, outward),
        out_shape=out_shape,
        in_specs=in_specs,
        out_specs=[vmem] * len(out_shape),
        scratch_shapes=[pltpu.VMEM(near.shape, jnp.int32)]
        + [f32(block_shape)] * 5
        + [
            pltpu.VMEM(block_shape, jnp.int32),
            pltpu.SemaphoreType.DMA((7,)),
            f32(block_shape),
            f32((2,) + block_shape),
            f32((2,) + block_shape),
            f32((2,) + block_shape),
            f32((slots + 1, 2, 16, TILE)),
            pltpu.SMEM((blocks * NEAR + 2,), jnp.int32),
            pltpu.VMEM((2, TILE, 2 * LBLK), jnp.bfloat16),
            pltpu.VMEM((2, TILE, 2 * LBLK), jnp.bfloat16),
        ],
        compiler_params=pltpu.CompilerParams(vmem_limit_bytes=VMEM_BYTES),
        cost_estimate=pl.CostEstimate(
            flops=2_000_000_000 * (2 if outward else 1), bytes_accessed=200_000, transcendentals=0
        ),
        name="outward_pairs" if outward else "own_pairs",
    )(*args)


def gram_kernel(points, all_ref, own_ref, amounts_ref, factor_ref, noise_ref, transmit_ref, out_ref):
    cross = all_ref[...]
    depth = jnp.dot(
        amounts_ref[...], cross, precision=HIGH, preferred_element_type=jnp.float32
    )
    passed = jnp.exp(-depth)
    transmit_ref[...] = passed
    weight = passed * passed / noise_ref[...] * (1.0 / points)
    own = own_ref.shape[0]
    for a in range(own):
        scaled = weight * own_ref[a : a + 1, :]
        gram = lax.dot_general(
            scaled,
            cross,
            (((1,), (1,)), ((), ())),
            precision=HIGH,
            preferred_element_type=jnp.float32,
        )
        out_ref[a] = gram * factor_ref[a]


def gram_parts(points, cross_all, cross_own, amounts, factor, noise):
    sounds, columns = amounts.shape
    width = noise.shape[0]
    vmem = pl.BlockSpec(memory_space=pltpu.VMEM)
    return pl.pallas_call(
        functools.partial(gram_kernel, points),
        out_shape=(
            jax.ShapeDtypeStruct((sounds, width), jnp.float32),
            jax.ShapeDtypeStruct(factor.shape, jnp.float32),
        ),
        in_specs=[vmem] * 5,
        out_specs=[vmem] * 2,
        compiler_params=pltpu.CompilerParams(vmem_limit_bytes=VMEM_BYTES),
        name="gram_parts",
    )(cross_all, cross_own, amounts, factor, noise.reshape(1, -1))


def body(
    line_offset,
    line_strength,
    lower_energy,
    lorentz_width,
    doppler_width,
    line_species,
    cutoff,
    layer_pressure,
    layer_temp,
    column_index,
    column_table,
    noise_var,
):
    groups = lax.axis_size(GROUP)
    place = jnp.stack([lax.axis_index(GROUP), lax.axis_index("lay")]).astype(jnp.int32)
    lines = (
        line_offset,
        line_strength,
        lower_energy,
        lorentz_width,
        doppler_width,
        line_species,
    )
    shared = (place, cutoff, layer_pressure, layer_temp, lines)
    lower_part, upper_part = pair_sums(True, *shared)
    from_above = passed_along(lower_part, -1)
    from_below = passed_along(upper_part, 1)
    middle, amounts, factor = pair_sums(False, *shared, column_index, column_table)
    cross_own = middle + from_above + from_below
    cross_all = lax.all_gather(cross_own, "lay", axis=0, tiled=True)
    points = noise_var.shape[0] * groups
    transmit, partial = gram_parts(points, cross_all, cross_own, amounts, factor, noise_var)
    flat = partial.reshape(-1, 128)
    stride = 1
    while stride < groups:
        size = min(8, groups // stride)
        copies = jnp.broadcast_to(flat[None], (size,) + flat.shape)
        flat = summed_over(copies, groups, size, stride)
        stride *= size
    normals = flat.reshape(partial.shape).transpose(1, 0, 2)
    return (transmit, normals)


def solution(mesh):
    in_specs = (
        P(GROUP),
        P(GROUP),
        P(GROUP),
        P(GROUP),
        P(GROUP),
        P(GROUP),
        P(GROUP, None),
        P("lay"),
        P("lay"),
        P(),
        P(),
        P(GROUP),
    )
    out_specs = (P(None, GROUP), P(None, "lay", None))
    return jax.shard_map(body, mesh=mesh, in_specs=in_specs, out_specs=out_specs, check_vma=False)
```

time: 101 us -> 72.7 us (0.72)
  matrix products: 39.3 us -> 0 us
  Pallas kernels: 0 us -> 22.9 us
  other arithmetic: 8.97 us -> 0.12 us
  blocking collectives: 41.7 us -> 38 us
  local copies, waits for them, and re-layouts: 2.98 us -> 4.68 us
    dot_general x5 -> x0, matrix products: 39.3 us -> none  [the longest x1 35.8 us: block_terms(): tile_terms = jnp.einsum('lsk,jlkp->jlsp', weights, profile, precision=HIGH)]
    pallas_call x0 -> x3, Pallas kernels: none -> 22.9 us  [the longest x2 22 us: pair_sums(): pl.pallas_call(functools.partial(pairs_kernel, outward), out_shape=out_sh...]
    mul x4 -> x0, other arithmetic: 5.52 us -> none  [the longest x1 4.6 us: profile_shape(): distance * distance + half_width * half_width]
    all_to_all x2, blocking collectives: 34.8 us -> 31 us  [summed_over(): lax.all_to_all(copies, GROUP, 0, 0, axis_index_groups=members, tiled=True)]
    unnamed x12 -> x32, local copies, waits for them, and re-layouts: 1.56 us -> 4.35 us
  transfers between devices with their start and end apart: 2 -> 2, of which waited for: 1 -> 0; matrix products, arithmetic and copies ran while one was open for 0% -> 0% of each run, Pallas kernels for 0% -> 14%
where the time goes in v2:
time: 72.7 us; the launch traced here: 72.4 us
  blocking collectives  38 us (52%)
  Pallas kernels  22.9 us (31%)
  starting transfers between devices  5.84 us (8%)
  local copies, waits for them, and re-layouts  4.68 us (6%)
  between operations  0.81 us (1%)
    all_to_all x2, blocking collectives, summed_over(): lax.all_to_all(copies, GROUP, 0, 0, axis_index_groups=members, tiled=True)  31 us
    pallas_call x2, Pallas kernels, pair_sums(): pl.pallas_call(functools.partial(pairs_kernel, outward), out_shape=out_sh...  22 us
    all_gather x1, blocking collectives, body(): cross_all = lax.all_gather(cross_own, 'lay', axis=0, tiled=True)  6.93 us
    ppermute x2, starting transfers between devices, passed_along(): return lax.ppermute(value, GROUP, pairs)  5.84 us
    unnamed x32, local copies, waits for them, and re-layouts  4.35 us
  transfers between devices with their start and end apart: 2, of which 0 were waited for; matrix products, arithmetic and copies ran while one was open for 0% of the time, Pallas kernels for 14%

profile of v2, /device:TPU:4, one launch (start us, length us, event | category | flops | bytes accessed | tf_op | source)
XLA Modules:
  0.0 72.4 jit_solution(9699950005897515503)
XLA Ops:
  0.7 0.6 copy-done.13
  1.3 0.1 copy.33.near_hbm
  1.4 0.1 reshape.40.near_ref
  1.5 0.1 pad_add_fusion.place_ref
  1.6 0.4 copy-done.3
  2.0 0.1 copy-done.1
  2.1 0.0 copy-done.2
  2.1 0.1 copy-done.10
  2.3 0.7 copy-done.5
  3.0 0.7 copy-done.7
  3.7 11.5 %outward_pairs.1 = (f32[6,1024]{1,0:T(8,128)S(1)}, f32[6,1024]{1,0:T(8,128)S(1)}) custom-call(s32[2]{0:T(128)S(1)} %pad_add_fusion.place_ref, s32[128]{0:T(128)S(1)} %reshape.40.near_ref, f32[2]{0:T(128)S(1)} %copy-done.10, f32[2]{0:T(128)S(1)} %copy-done.11, s32[32,4]{1,0:T(8,128)S(1)} %copy.33.near_hbm, f32[32,128]{1,0:T(8,128)S(1)} %bitcast.13, ...), custom_call_target="tpu_custom_call" | custom-call | flops 4000000000 | bytes 200000 | tf_op jit(solution)/shard_map/outward_pairs/pallas_call | solution.py:285
  15.3 1.3 %collective-permute-start = (f32[6,1024]{1,0:T(8,128)S(1)}, f32[6,1024]{1,0:T(8,128)S(1)}, u32[]{:S(2)}, u32[]{:S(2)}) collective-permute-start(f32[6,1024]{1,0:T(8,128)S(1)} %get-tuple-element.10), channel_id=1, source_target_pairs={{4,0},{8,4},{12,8},{16,12},{20,16},{24,20},{28,24},{32,28},{36,32}... | collective-permute-start | bytes 73736 | tf_op jit(solution)/shard_map/ppermute | solution.py:27
  16.6 0.0 copy-start.9
  16.6 4.5 %collective-permute-start.1 = (f32[6,1024]{1,0:T(8,128)S(1)}, f32[6,1024]{1,0:T(8,128)S(1)}, u32[]{:S(2)}, u32[]{:S(2)}) collective-permute-start(f32[6,1024]{1,0:T(8,128)S(1)} %get-tuple-element.11), channel_id=1, source_target_pairs={{0,4},{4,8},{8,12},{12,16},{16,20},{20,24},{24,28},{28,32},{32,36}... | collective-permute-start | bytes 73736 | tf_op jit(solution)/shard_map/ppermute | solution.py:27
  21.1 0.1 copy.35.rest_0_
  21.2 10.4 %own_pairs.1 = (f32[6,1024]{1,0:T(8,128)S(1)}, f32[32,24]{1,0:T(8,128)S(1)}, f32[6,32,24]{2,1,0:T(8,128)S(1)}) custom-call(s32[2]{0:T(128)S(1)} %pad_add_fusion.place_ref, s32[128]{0:T(128)S(1)} %reshape.40.near_ref, f32[2]{0:T(128)S(1)} %copy-done.10, f32[2]{0:T(128)S(1)} %copy-done.11, s32[32,4]{1,0:T(8,128)S(1)} %copy.33.near_hbm, ...), custom_call_target="tpu_custom_call" | custom-call | flops 2000000000 | bytes 200000 | tf_op jit(solution)/shard_map/own_pairs/pallas_call | solution.py:285
  31.7 6.9 %all-gather = f32[4,6,1024]{2,1,0:T(8,128)S(1)} all-gather(f32[1,6,1024]{2,1,0:T(8,128)S(1)} %bitcast.11), channel_id=1, replica_groups=mesh['spec'=16,'line'=4,'lay'=4] {'lay'}, dimensions={0}, use_global_device_ids=true | all-gather | bytes 122880 | tf_op jit(solution)/shard_map/all_gather | solution.py:380
  38.7 0.7 copy-done
  39.3 1.0 %gram_parts.1 = (f32[32,1024]{1,0:T(8,128)}, f32[6,32,24]{2,1,0:T(8,128)S(1)}) custom-call(f32[24,1024]{1,0:T(8,128)S(1)} %reshape.50.all_ref, f32[6,1024]{1,0:T(8,128)S(1)} %add_add_fusion.own_ref, f32[32,24]{1,0:T(8,128)S(1)} %get-tuple-element.12.amounts_ref, f32[6,32,24]{2,1,0:T(8,128)S(1)} %get-tuple-element.13.factor_ref, f32[1,1024]{1,0:T(1,128)S(1)} %bitcast.12), custom_call_target="tpu_custom_call" | custom-call | tf_op jit(solution)/shard_map/gram_parts/pallas_call | solution.py:337
  40.3 0.1 broadcast_in_dim.6
  40.4 11.0 %all_to_all.10 = f32[8,36,128]{2,1,0:T(8,128)S(1)} all-to-all(f32[8,36,128]{2,1,0:T(8,128)S(1)} %broadcast_in_dim.14), channel_id=1, replica_groups={{0,4,8,12,16,20,24,28},{32,36,40,44,48,52,56,60},{64,68,72,76,80,84,88,..., dimensions={0} | all-to-all | bytes 294912 | tf_op jit(solution)/shard_map/all_to_all | solution.py:36
  51.5 20.0 %all_to_all.11 = f32[8,36,128]{2,1,0:T(8,128)S(1)} all-to-all(f32[8,36,128]{2,1,0:T(8,128)S(1)} %broadcast_in_dim.15), channel_id=1, replica_groups={{0,32,64,96,128,160,192,224},{4,36,68,100,132,164,196,228},{8,40,72,104..., dimensions={0} | all-to-all | bytes 294912 | tf_op jit(solution)/shard_map/all_to_all | solution.py:36
  71.5 0.1 reshape.48
  71.6 0.7 copy.39
  (27 shorter events, 0.1 us)
Async XLA Ops:
  0.6 0.7 copy-start.13
  0.6 1.0 %copy-start.11 = (f32[2]{0:T(128)S(1)}, f32[2]{0:T(128)}, u32[]{:S(2)}) copy-start(f32[2]{0:T(128)} %temper_ref.3) | copy-start | bytes 28
  0.7 0.9 %copy-start.4 = (f32[4096]{0:T(1024)S(1)}, f32[4096]{0:T(1024)}, u32[]{:S(2)}) copy-start(f32[4096]{0:T(1024)} %param.15) | copy-start | bytes 49156
  1.3 0.7 copy-start.3
  1.4 0.7 copy-start.1
  1.4 0.7 %copy-start.2 = (f32[4096]{0:T(1024)S(1)}, f32[4096]{0:T(1024)}, u32[]{:S(2)}) copy-start(f32[4096]{0:T(1024)} %param.13) | copy-start | bytes 49156
  1.6 0.7 copy-start.10
  2.3 0.7 copy-start.5
  3.0 0.7 copy-start.7
  3.7 17.4 %copy-start.12 = (s32[32,8]{0,1:T(8,128)S(1)}, s32[32,8]{0,1:T(8,128)}, u32[]{:S(2)}) copy-start(s32[32,8]{0,1:T(8,128)} %param.21) | copy-start | bytes 3076
  3.7 17.5 %copy-start.8 = (s32[4096]{0:T(1024)S(1)}, s32[4096]{0:T(1024)}, u32[]{:S(2)}) copy-start(s32[4096]{0:T(1024)} %param.17) | copy-start | bytes 49156
  15.3 6.0 %copy-start.6 = (f32[4096]{0:T(1024)S(1)}, f32[4096]{0:T(1024)}, u32[]{:S(2)}) copy-start(f32[4096]{0:T(1024)} %param.16) | copy-start | bytes 49156
  15.3 16.4 %collective-permute-start = (f32[6,1024]{1,0:T(8,128)S(1)}, f32[6,1024]{1,0:T(8,128)S(1)}, u32[]{:S(2)}, u32[]{:S(2)}) collective-permute-start(f32[6,1024]{1,0:T(8,128)S(1)} %get-tuple-element.10), channel_id=1, source_target_pairs={{4,0},{8,4},{12,8},{16,12},{20,16},{24,20},{28,24},{32,28},{36,32}... | collective-permute-start | bytes 73736 | tf_op jit(solution)/shard_map/ppermute | solution.py:27
  16.6 4.7 %copy-start.9 = (f32[3,64]{1,0:T(4,128)S(1)}, f32[3,64]{1,0:T(4,128)}, u32[]{:S(2)}) copy-start(f32[3,64]{1,0:T(4,128)} %rest_1_.1) | copy-start | bytes 2308
  16.6 15.1 %collective-permute-start.1 = (f32[6,1024]{1,0:T(8,128)S(1)}, f32[6,1024]{1,0:T(8,128)S(1)}, u32[]{:S(2)}, u32[]{:S(2)}) collective-permute-start(f32[6,1024]{1,0:T(8,128)S(1)} %get-tuple-element.11), channel_id=1, source_target_pairs={{0,4},{4,8},{8,12},{12,16},{16,20},{20,24},{24,28},{28,32},{32,36}... | collective-permute-start | bytes 73736 | tf_op jit(solution)/shard_map/ppermute | solution.py:27
  38.6 0.7 copy-start

commit v3 on v0

v3 whole, which is shorter than its diff:
```python
import functools
import math

import jax
import jax.numpy as jnp
from jax import lax
from jax.experimental import pallas as pl
from jax.experimental.pallas import tpu as pltpu
from jax.sharding import PartitionSpec as P

TILE = 256
LBLK = 128
NEAR = 4
SPECIES = 3
OWN_TILES = 4
HOME_BATCH = 4
AWAY_BATCH = 2
GROUP = ("spec", "line")

HIGH = lax.Precision.HIGHEST
LN_TWO = math.log(2.0)
C_TWO = 1.4388
VMEM_BYTES = 40 * 1024 * 1024


def exchanged(value, start):
    peers = lax.axis_size(GROUP)
    pairs = [(i, i + 1) for i in range(start, peers - 1, 2)]
    return lax.ppermute(value, GROUP, pairs + [(j, i) for i, j in pairs])


def summed_over(copies, total, size, stride):
    members = [
        [base + stride * k for k in range(size)]
        for base in range(total)
        if (base // stride) % size == 0
    ]
    landed = lax.all_to_all(copies, GROUP, 0, 0, axis_index_groups=members, tiled=True)
    return jnp.sum(landed, axis=0)


def line_tables(press, temper, strength, energy, lwidth, dwidth, rate_ref, mix_ref, amp_ref):
    shape = strength.shape
    for layer in range(2):
        temp = jnp.broadcast_to(temper[:, layer : layer + 1], shape)
        pressure = jnp.broadcast_to(press[:, layer : layer + 1], shape)
        ratio = 296.0 / temp
        lor = lwidth * (pressure * jnp.exp(0.75 * jnp.log(ratio)))
        gau = dwidth * jnp.sqrt(temp / 296.0)
        line = strength * jnp.exp(-C_TWO * energy * (1.0 / temp - 1.0 / 296.0))
        g2 = gau * gau
        g4 = g2 * g2
        l2 = lor * lor
        l4 = l2 * l2
        total = (
            g4 * gau
            + 2.69269 * g4 * lor
            + 2.42843 * g2 * gau * l2
            + 4.47163 * g2 * lor * l2
            + 0.07842 * gau * l4
            + l4 * lor
        )
        width = jnp.exp(0.2 * jnp.log(total))
        inverse = 1.0 / width
        part = lor * inverse
        eta = part * (1.36603 + part * (-0.47719 + part * 0.11116))
        peak = eta * (2.0 / math.pi)
        rate_ref[layer] = -4.0 * inverse * inverse
        mix_ref[layer] = (1.0 - eta) * math.sqrt(4.0 * LN_TWO / math.pi) / peak
        amp_ref[layer] = line * peak * inverse


def own_place():
    return lax.axis_index(GROUP), lax.axis_index("lay")


def pairs_kernel(*refs):
    hbm, outs, scratch = refs[:9], refs[9:12], refs[12:]
    vmem, sems = scratch[:9], scratch[9]
    near, press_v, temper_v, offset_v, strength_v, energy_v, lwidth_v, dwidth_v, species_v = vmem
    rate_ref, mix_ref, amp_ref, point_ref, list_ref = scratch[10:15]
    home_acc, away_acc = scratch[15:17], scratch[17:19]
    home_bufs = scratch[19 : 19 + 2 * HOME_BATCH]
    away_bufs = home_bufs[: 2 * AWAY_BATCH]
    copies = [pltpu.make_async_copy(s, d, sems.at[i]) for i, (s, d) in enumerate(zip(hbm, vmem))]
    for copy in copies:
        copy.start()
    for acc in home_acc + away_acc:
        acc[...] = jnp.zeros_like(acc)
    point_ref[...] = lax.broadcasted_iota(jnp.int32, point_ref.shape, 0).astype(jnp.float32)

    slots = home_acc[0].shape[0] - 1
    blocks = near.shape[1]
    group = own_place()[0]
    base = (group - 1) * OWN_TILES
    copies[0].wait()
    pad = 2 * AWAY_BATCH
    for k in range(pad):
        list_ref[k] = jnp.int32(0)
    found = jnp.int32(pad)
    for b in range(blocks):
        for j in range(1, NEAR):
            list_ref[found] = jnp.int32(NEAR * b + j)
            found = found + (near[j, b] >= 0).astype(jnp.int32)
    for k in range(2 * pad):
        list_ref[found + k] = jnp.int32(0)

    for copy in copies[1:]:
        copy.wait()
    line_tables(
        press_v[...],
        temper_v[...],
        strength_v[...],
        energy_v[...],
        lwidth_v[...],
        dwidth_v[...],
        rate_ref,
        mix_ref,
        amp_ref,
    )

    lane = lax.broadcasted_iota(jnp.int32, (1, LBLK), 1)
    lane_three = lax.rem(lane, 3)
    home_row = lax.broadcasted_iota(jnp.int32, (NEAR * 8, LBLK), 0)
    home_part = home_row & 7
    home_rest = home_part >= SPECIES
    home_key = jnp.where(
        home_part < 2 * SPECIES, home_row - jnp.where(home_rest, SPECIES, 0), -1
    )
    away_key = lax.broadcasted_iota(jnp.int32, (NEAR * 4, LBLK), 0)
    upper_half = lax.broadcasted_iota(jnp.int32, (8, TILE), 0) >= 4

    def entries(b):
        tiles = [near[j, b] for j in range(NEAR)]
        count = jnp.int32(1)
        for j in range(1, NEAR):
            count = count + (tiles[j] >= 0).astype(jnp.int32)
        own = jnp.where(count == 3, lane_three, lane & jnp.where(count == 4, 3, count - 1))
        return tiles, count, own

    def rotated(own, count, r):
        entry = own + r
        return jnp.where(entry >= count, entry - count, entry)

    def chosen(entry, tiles):
        tile = jnp.where(entry == 0, tiles[0], tiles[NEAR - 1])
        for j in range(1, NEAR - 1):
            tile = jnp.where(entry == j, tiles[j], tile)
        return tile

    def evaluate(b, shift, buf, at, split):
        shape = (16, LBLK)
        shift = jnp.broadcast_to(shift, shape)
        rate = [jnp.broadcast_to(rate_ref[layer, pl.ds(b, 1), :], shape) for layer in range(2)]
        mix = [jnp.broadcast_to(mix_ref[layer, pl.ds(b, 1), :], shape) for layer in range(2)]
        for k in range(0, TILE, 16):
            x = point_ref[k : k + 16, :] + shift
            square = x * x
            for layer in range(2):
                q = square * rate[layer]
                value = 1.0 / (1.0 - q) + mix[layer] * jnp.exp2(q)
                high = value.astype(jnp.bfloat16)
                buf[layer, k : k + 16, at : at + LBLK] = high
                if split:
                    buf[layer, k : k + 16, LBLK:] = (value - high.astype(jnp.float32)).astype(
                        jnp.bfloat16
                    )

    def times(left, right):
        return lax.dot_general(
            left, right, (((1,), (1,)), ((), ())), preferred_element_type=jnp.float32
        )

    def slot_of(tile, live):
        return jnp.where(live & (tile >= 0), tile - base, slots)

    def home_evaluate(b, buf):
        evaluate(b, -offset_v[pl.ds(b, 1), :], buf, 0, True)

    def home_reduce(b, buf):
        live = b >= 0
        b = jnp.maximum(b, 0)
        tiles, _, own = entries(b)
        hit = home_key == own * 8 + species_v[pl.ds(b, 1), :]
        for layer in range(2):
            amp = jnp.broadcast_to(amp_ref[layer, pl.ds(b, 1), :], home_row.shape)
            high = amp.astype(jnp.bfloat16).astype(jnp.float32)
            part = jnp.where(home_rest, amp - high, high)
            left = jnp.where(hit, part, 0.0).astype(jnp.bfloat16)
            sums = times(jnp.concatenate([left, left], axis=1), buf[layer])
            for j in range(NEAR):
                home_acc[layer][slot_of(tiles[j], live)] += sums[8 * j : 8 * j + 8]

    def decode(i):
        code = list_ref[i]
        return lax.shift_right_logical(code, 2), code & 3

    def away_evaluate(i, buf):
        for k in range(2):
            b, r = decode(2 * i + k)
            tiles, count, own = entries(b)
            apart = chosen(rotated(own, count, r), tiles) - chosen(own, tiles)
            shift = (apart * TILE).astype(jnp.float32) - offset_v[pl.ds(b, 1), :]
            evaluate(b, shift, buf, k * LBLK, False)

    def away_reduce(i, buf):
        items = []
        for k in range(2):
            b, r = decode(2 * i + k)
            tiles, count, own = entries(b)
            key = rotated(own, count, r) * 4 + species_v[pl.ds(b, 1), :]
            items.append((b, away_key == key, [slot_of(tile, r > 0) for tile in tiles]))
        empty = jnp.zeros(away_key.shape, jnp.bfloat16)
        for layer in range(2):
            left = [
                jnp.where(
                    hit, jnp.broadcast_to(amp_ref[layer, pl.ds(b, 1), :], away_key.shape), 0.0
                ).astype(jnp.bfloat16)
                for b, hit, _ in items
            ]
            stacked = jnp.concatenate(
                [
                    jnp.concatenate([left[0], empty], axis=1),
                    jnp.concatenate([empty, left[1]], axis=1),
                ],
                axis=0,
            )
            sums = times(stacked, buf[layer])
            for k, (_, _, slot) in enumerate(items):
                for j in range(NEAR):
                    at = 16 * k + 8 * (j // 2)
                    part = sums[at : at + 8]
                    part = jnp.where(upper_half, part, 0.0) if j % 2 else jnp.where(upper_half, 0.0, part)
                    away_acc[layer][slot[j]] += part

    def alternate(batch, bufs, evaluate_one, reduce_one, turns):
        def step(i, carry):
            at = 2 * batch * i
            for k in range(batch):
                evaluate_one(at + k, bufs[k])
            for k in range(batch):
                reduce_one(at - batch + k, bufs[batch + k])
            for k in range(batch):
                evaluate_one(at + batch + k, bufs[batch + k])
            for k in range(batch):
                reduce_one(at + k, bufs[k])
            return carry

        lax.fori_loop(0, turns, step, 0)
        for k in range(batch):
            reduce_one(2 * batch * turns - batch + k, bufs[batch + k])

    alternate(
        HOME_BATCH, home_bufs, home_evaluate, home_reduce, jnp.int32(blocks // (2 * HOME_BATCH))
    )
    span = 4 * AWAY_BATCH
    alternate(
        AWAY_BATCH,
        away_bufs,
        lambda i, buf: away_evaluate(i + AWAY_BATCH, buf),
        lambda i, buf: away_reduce(i + AWAY_BATCH, buf),
        lax.div(found - pad + span - 1, span),
    )

    even = (group & 1) == 0
    for slot in range(OWN_TILES):
        at = slot * TILE
        for layer in range(2):
            parts = []
            for third in range(3):
                home = home_acc[layer][third * OWN_TILES + slot]
                away = away_acc[layer][third * OWN_TILES + slot]
                parts.append(
                    home[:SPECIES]
                    + home[SPECIES : 2 * SPECIES]
                    + (away[:SPECIES] + away[4 : 4 + SPECIES])
                )
            where = (slice(SPECIES * layer, SPECIES * (layer + 1)), slice(at, at + TILE))
            outs[0][where] = jnp.where(even, parts[2], parts[0])
            outs[1][where] = parts[1]
            outs[2][where] = jnp.where(even, parts[0], parts[2])


def pair_sums(near, press, temper, lines):
    blocks = near.shape[1]
    row_count = 2 * SPECIES
    vmem = pl.BlockSpec(memory_space=pltpu.VMEM)
    hbm = pl.BlockSpec(memory_space=pltpu.HBM)
    block_shape = (blocks, LBLK)
    f32 = functools.partial(pltpu.VMEM, dtype=jnp.float32)
    sums = jax.ShapeDtypeStruct((row_count, OWN_TILES * TILE), jnp.float32)
    return pl.pallas_call(
        pairs_kernel,
        out_shape=(sums,) * 3,
        in_specs=[hbm] * 9,
        out_specs=[vmem] * 3,
        scratch_shapes=[pltpu.SMEM(near.shape, jnp.int32), f32((1, 2)), f32((1, 2))]
        + [f32(block_shape)] * 5
        + [
            pltpu.VMEM(block_shape, jnp.int32),
            pltpu.SemaphoreType.DMA((9,)),
            f32((2,) + block_shape),
            f32((2,) + block_shape),
            f32((2,) + block_shape),
            f32((TILE, LBLK)),
            pltpu.SMEM((blocks * (NEAR - 1) + 6 * AWAY_BATCH,), jnp.int32),
        ]
        + [f32((3 * OWN_TILES + 1, 8, TILE))] * 4
        + [pltpu.VMEM((2, TILE, 2 * LBLK), jnp.bfloat16)] * (2 * HOME_BATCH),
        name="pair_sums",
    )(near, press.reshape(1, 2), temper.reshape(1, 2), *[v.reshape(block_shape) for v in lines])


def amounts_kernel(
    points, index_ref, table_ref, noise_ref, sums_ref, amounts_ref, factor_ref, scale_ref, out_ref
):
    out_ref[...] = sums_ref[...]
    scale_ref[...] = (1.0 / points) / noise_ref[...]
    layers, sounds = index_ref.shape
    kinds, entries = table_ref.shape
    entry = lax.broadcasted_iota(jnp.int32, (entries, sounds), 0)
    for layer in range(layers):
        hit = (entry == index_ref[layer : layer + 1, :]).astype(jnp.float32)
        amounts_ref[kinds * layer : kinds * (layer + 1), :] = jnp.dot(
            table_ref[...], hit, precision=HIGH, preferred_element_type=jnp.float32
        )
    amounts = amounts_ref[...]
    own = factor_ref.shape[0]
    first = own * own_place()[1]
    for a in range(own):
        factor_ref[a] = amounts * amounts_ref[pl.ds(first + a, 1), :]


def amount_tables(points, index, table, noise, sums):
    layers, sounds = index.shape
    columns = layers * SPECIES
    vmem = pl.BlockSpec(memory_space=pltpu.VMEM)
    return pl.pallas_call(
        functools.partial(amounts_kernel, points),
        out_shape=(
            jax.ShapeDtypeStruct((columns, sounds), jnp.float32),
            jax.ShapeDtypeStruct((2 * SPECIES, columns, sounds), jnp.float32),
            jax.ShapeDtypeStruct((1, noise.shape[0]), jnp.float32),
            jax.ShapeDtypeStruct(sums.shape, jnp.float32),
        ),
        in_specs=[vmem] * 4,
        out_specs=[vmem] * 4,
        compiler_params=pltpu.CompilerParams(vmem_limit_bytes=VMEM_BYTES),
        cost_estimate=pl.CostEstimate(flops=2_000_000, bytes_accessed=100_000, transcendentals=0),
        name="amount_tables",
    )(index, table, noise.reshape(1, -1), sums)


def gram_kernel(all_ref, amounts_ref, factor_ref, scale_ref, transmit_ref, out_ref):
    lays, own = all_ref.shape[:2]
    cross = jnp.concatenate([all_ref[i] for i in range(lays)], axis=0)
    depth = lax.dot_general(
        amounts_ref[...],
        cross,
        (((0,), (0,)), ((), ())),
        precision=HIGH,
        preferred_element_type=jnp.float32,
    )
    passed = jnp.exp(-depth)
    transmit_ref[...] = passed
    weight = passed * passed * scale_ref[...]
    lay = own_place()[1]
    for a in range(own):
        scaled = weight * all_ref[lay, a : a + 1, :]
        gram = lax.dot_general(
            cross,
            scaled,
            (((1,), (1,)), ((), ())),
            precision=HIGH,
            preferred_element_type=jnp.float32,
        )
        out_ref[a] = gram * factor_ref[a]


def gram_parts(cross_all, amounts, factor, scale):
    sounds = amounts.shape[1]
    width = scale.shape[1]
    vmem = pl.BlockSpec(memory_space=pltpu.VMEM)
    return pl.pallas_call(
        gram_kernel,
        out_shape=(
            jax.ShapeDtypeStruct((sounds, width), jnp.float32),
            jax.ShapeDtypeStruct(factor.shape, jnp.float32),
        ),
        in_specs=[vmem] * 4,
        out_specs=[vmem] * 2,
        compiler_params=pltpu.CompilerParams(vmem_limit_bytes=VMEM_BYTES),
        name="gram_parts",
    )(cross_all, amounts, factor, scale)


def body(
    line_offset,
    line_strength,
    lower_energy,
    lorentz_width,
    doppler_width,
    line_species,
    cutoff,
    layer_pressure,
    layer_temp,
    column_index,
    column_table,
    noise_var,
):
    groups = lax.axis_size(GROUP)
    lines = (
        line_offset,
        line_strength,
        lower_energy,
        lorentz_width,
        doppler_width,
        line_species,
    )
    first, middle, second = pair_sums(cutoff.T, layer_pressure, layer_temp, lines)
    landed = [exchanged(first, 0), exchanged(second, 1)]
    points = noise_var.shape[0] * groups
    amounts, factor, scale, middle = amount_tables(
        points, column_index.T, column_table, noise_var, middle
    )
    cross_own = middle + landed[0] + landed[1]
    cross_all = lax.all_gather(cross_own, "lay", axis=0)
    transmit, partial = gram_parts(cross_all, amounts, factor, scale)
    flat = partial.reshape(-1, 128)
    stride = 1
    while stride < groups:
        size = min(8, groups // stride)
        copies = jnp.broadcast_to(flat[None], (size,) + flat.shape)
        flat = summed_over(copies, groups, size, stride)
        stride *= size
    normals = flat.reshape(partial.shape).transpose(2, 0, 1)
    return (transmit, normals)


def solution(mesh):
    in_specs = (
        P(GROUP),
        P(GROUP),
        P(GROUP),
        P(GROUP),
        P(GROUP),
        P(GROUP),
        P(GROUP, None),
        P("lay"),
        P("lay"),
        P(),
        P(),
        P(GROUP),
    )
    out_specs = (P(None, GROUP), P(None, "lay", None))
    return jax.shard_map(body, mesh=mesh, in_specs=in_specs, out_specs=out_specs, check_vma=False)
```

time: 462 us -> 63 us (0.14)
  blocking collectives: 317 us -> 41.7 us
  waiting for transfers between devices: 45 us -> 1.63 us
  matrix products: 39.5 us -> 0 us
  local copies, waits for them, and re-layouts: 31.8 us -> 1.6 us
  Pallas kernels: 0 us -> 15 us
  between operations: 14.3 us -> 0.74 us
  other arithmetic: 8.27 us -> 0.04 us
    psum x1 -> x0, blocking collectives: 310 us -> none  [body(): normals = lax.psum(partial_normals, ('spec', 'line'))]
    psum x1 -> x0, waiting for transfers between devices: 44 us -> none  [body(): optical_depth = lax.psum(local_depth, 'lay')]
    dot_general x5 -> x0, matrix products: 39.5 us -> none  [the longest x1 36 us: block_terms(): tile_terms = jnp.einsum('lsk,jlkp->jlsp', weights, profile, precision=HIGH)]
    all_to_all x0 -> x2, blocking collectives: none -> 34.8 us  [summed_over(): lax.all_to_all(copies, GROUP, 0, 0, axis_index_groups=members, tiled=True)]
    gather x1 -> x0, local copies, waits for them, and re-layouts: 29.9 us -> none  [block_terms(): home_tile = near_list[slot_index]]
    pallas_call x0 -> x3, Pallas kernels: none -> 15 us  [the longest x1 13.7 us: pair_sums(): pl.pallas_call(pairs_kernel, out_shape=(sums,) * 3, in_specs=[hbm] * 9, o...]
  transfers between devices with their start and end apart: 3 -> 2, of which waited for: 2 -> 1; matrix products, arithmetic and copies ran while one was open for 0% -> 0% of each run, Pallas kernels for 0% -> 1%
where the time goes in v3:
time: 63 us; the launch traced here: 62.2 us
  blocking collectives  41.7 us (66%)
  Pallas kernels  15 us (24%)
  waiting for transfers between devices  1.63 us (3%)
  local copies, waits for them, and re-layouts  1.6 us (3%)
  starting transfers between devices  1.46 us (2%)
  between operations  0.74 us (1%)
    all_to_all x2, blocking collectives, summed_over(): lax.all_to_all(copies, GROUP, 0, 0, axis_index_groups=members, tiled=True)  34.8 us
    pallas_call x1, Pallas kernels, pair_sums(): pl.pallas_call(pairs_kernel, out_shape=(sums,) * 3, in_specs=[hbm] * 9, o...  13.7 us
    all_gather x1, blocking collectives, body(): cross_all = lax.all_gather(cross_own, 'lay', axis=0)  6.93 us
    ppermute x2, waiting for transfers between devices, exchanged(): return lax.ppermute(value, GROUP, pairs + [(j, i) for i, j in pairs])  1.63 us
    ppermute x2, starting transfers between devices, exchanged(): return lax.ppermute(value, GROUP, pairs + [(j, i) for i, j in pairs])  1.46 us
  transfers between devices with their start and end apart: 2, of which 1 were waited for; matrix products, arithmetic and copies ran while one was open for 0% of the time, Pallas kernels for 1%

profile of v3, /device:TPU:4, one launch (start us, length us, event | category | flops | bytes accessed | tf_op | source)
XLA Modules:
  0.0 62.2 jit_solution(9522599279406012914)
XLA Ops:
  0.6 0.0 copy-start.3
  0.6 13.7 %pair_sums.1 = (f32[6,1024]{1,0:T(8,128)}, f32[6,1024]{1,0:T(8,128)}, f32[6,1024]{1,0:T(8,128)}) custom-call(s32[4,32]{1,0:T(4,128)} %bitcast.23, f32[1,2]{1,0:T(1,128)} %bitcast.24, f32[1,2]{1,0:T(1,128)} %bitcast.25, f32[32,128]{1,0:T(8,128)} %bitcast.17, f32[32,128]{1,0:T(8,128)} %bitcast.18, f32[32,128]{1,0:T(8,128)} %bitcast.19, f32[32,128]{1,0:T(8,128)} %bitcast.20, ...), custom_call_target="tpu_custom_call" | custom-call | tf_op jit(solution)/shard_map/pair_sums/pallas_call | solution.py:292
  14.4 0.0 copy-start.2
  14.4 0.0 copy-start.1
  14.4 0.8 %collective-permute-start = (f32[6,1024]{1,0:T(8,128)}, f32[6,1024]{1,0:T(8,128)S(1)}, u32[]{:S(2)}, u32[]{:S(2)}) collective-permute-start(f32[6,1024]{1,0:T(8,128)} %get-tuple-element.13), channel_id=1, source_target_pairs={{0,4},{8,12},{16,20},{24,28},{32,36},{40,44},{48,52},{56,60},{64,6... | collective-permute-start | bytes 73736 | tf_op jit(solution)/shard_map/ppermute | solution.py:29
  15.2 0.7 %collective-permute-start.1 = (f32[6,1024]{1,0:T(8,128)}, f32[6,1024]{1,0:T(8,128)S(1)}, u32[]{:S(2)}, u32[]{:S(2)}) collective-permute-start(f32[6,1024]{1,0:T(8,128)} %get-tuple-element.14), channel_id=1, source_target_pairs={{4,8},{12,16},{20,24},{28,32},{36,40},{44,48},{52,56},{60,64},{68,... | collective-permute-start | bytes 73736 | tf_op jit(solution)/shard_map/ppermute | solution.py:29
  15.9 0.0 copy-done.3
  15.9 0.0 copy-done.2
  15.9 0.0 copy-done.1
  15.9 0.0 copy-start
  15.9 0.7 %copy-done = f32[6,1024]{1,0:T(8,128)S(1)} copy-done((f32[6,1024]{1,0:T(8,128)S(1)}, f32[6,1024]{1,0:T(8,128)}, u32[]{:S(2)}) %copy-start) | copy-done | bytes 24600
  16.6 0.3 amount_tables.1
  17.0 1.6 %collective-permute-done = f32[6,1024]{1,0:T(8,128)S(1)} collective-permute-done((f32[6,1024]{1,0:T(8,128)}, f32[6,1024]{1,0:T(8,128)S(1)}, u32[]{:S(2)}, u32[]{:S(2)}) %collective-permute-start) | collective-permute-done | bytes 24608 | tf_op jit(solution)/shard_map/ppermute | solution.py:29
  18.6 0.0 collective-permute-done.1
  18.6 6.9 %all-gather.1.all_ref = f32[4,6,1024]{2,1,0:T(8,128)S(1)} all-gather(f32[1,6,1024]{2,1,0:T(8,128)S(1)} %add_bitcast_fusion), channel_id=2, replica_groups=mesh['spec'=16,'line'=4,'lay'=4] {'lay'}, dimensions={0}, use_global_device_ids=true | all-gather | bytes 122880 | tf_op jit(solution)/shard_map/all_gather | solution.py:427
  25.5 1.0 %gram_parts.1 = (f32[32,1024]{1,0:T(8,128)}, f32[6,24,32]{2,1,0:T(8,128)S(1)}) custom-call(f32[4,6,1024]{2,1,0:T(8,128)S(1)} %all-gather.1.all_ref, f32[24,32]{1,0:T(8,128)S(1)} %get-tuple-element.15.amounts_ref, f32[6,24,32]{2,1,0:T(8,128)S(1)} %get-tuple-element.16.factor_ref, f32[1,1024]{1,0:T(1,128)S(1)} %get-tuple-element.17.scale_ref), custom_call_target="tpu_custom_call" | custom-call | tf_op jit(solution)/shard_map/gram_parts/pallas_call | solution.py:384
  26.5 0.1 broadcast_in_dim.6
  26.7 16.2 %all_to_all.10 = f32[8,36,128]{2,1,0:T(8,128)S(1)} all-to-all(f32[8,36,128]{2,1,0:T(8,128)S(1)} %broadcast_in_dim.14), channel_id=1, replica_groups={{0,4,8,12,16,20,24,28},{32,36,40,44,48,52,56,60},{64,68,72,76,80,84,88,..., dimensions={0} | all-to-all | bytes 294912 | tf_op jit(solution)/shard_map/all_to_all | solution.py:38
  42.9 18.6 %all_to_all.11 = f32[8,36,128]{2,1,0:T(8,128)S(1)} all-to-all(f32[8,36,128]{2,1,0:T(8,128)S(1)} %broadcast_in_dim.15), channel_id=1, replica_groups={{0,32,64,96,128,160,192,224},{4,36,68,100,132,164,196,228},{8,40,72,104..., dimensions={0} | all-to-all | bytes 294912 | tf_op jit(solution)/shard_map/all_to_all | solution.py:38
  61.5 0.7 %reshape.45 = f32[6,24,32]{2,1,0:T(8,128)} reshape(f32[36,128]{1,0:T(8,128)S(1)} %reduce_sum.19) | data formatting | bytes 36864 | tf_op jit(solution)/shard_map/reshape | solution.py:436
  (5 shorter events, 0.1 us)
Async XLA Ops:
  0.6 15.2 %copy-start.3 = (f32[3,64]{1,0:T(4,128)S(1)}, f32[3,64]{1,0:T(4,128)}, u32[]{:S(2)}) copy-start(f32[3,64]{1,0:T(4,128)} %table_ref.1) | copy-start | bytes 2308
  14.4 1.5 %copy-start.2 = (f32[1024]{0:T(1024)S(1)}, f32[1024]{0:T(1024)}, u32[]{:S(2)}) copy-start(f32[1024]{0:T(1024)} %param.23) | copy-start | bytes 12292
  14.4 1.5 %copy-start.1 = (s32[32,8]{0,1:T(8,128)S(1)}, s32[32,8]{0,1:T(8,128)}, u32[]{:S(2)}) copy-start(s32[32,8]{0,1:T(8,128)} %param.21) | copy-start | bytes 3076
  14.4 4.2 %collective-permute-start = (f32[6,1024]{1,0:T(8,128)}, f32[6,1024]{1,0:T(8,128)S(1)}, u32[]{:S(2)}, u32[]{:S(2)}) collective-permute-start(f32[6,1024]{1,0:T(8,128)} %get-tuple-element.13), channel_id=1, source_target_pairs={{0,4},{8,12},{16,20},{24,28},{32,36},{40,44},{48,52},{56,60},{64,6... | collective-permute-start | bytes 73736 | tf_op jit(solution)/shard_map/ppermute | solution.py:29
  15.2 3.4 %collective-permute-start.1 = (f32[6,1024]{1,0:T(8,128)}, f32[6,1024]{1,0:T(8,128)S(1)}, u32[]{:S(2)}, u32[]{:S(2)}) collective-permute-start(f32[6,1024]{1,0:T(8,128)} %get-tuple-element.14), channel_id=1, source_target_pairs={{4,8},{12,16},{20,24},{28,32},{36,40},{44,48},{52,56},{60,64},{68,... | collective-permute-start | bytes 73736 | tf_op jit(solution)/shard_map/ppermute | solution.py:29
  15.9 0.8 %copy-start = (f32[6,1024]{1,0:T(8,128)S(1)}, f32[6,1024]{1,0:T(8,128)}, u32[]{:S(2)}) copy-start(f32[6,1024]{1,0:T(8,128)} %get-tuple-element.11.sums_ref) | copy-start | bytes 73732

commit v4 on v3

--- a/solution.py
+++ b/solution.py
@@ -13,8 +13,9 @@
 NEAR = 4
 SPECIES = 3
 OWN_TILES = 4
-HOME_BATCH = 4
-AWAY_BATCH = 2
+HOME_BATCH = 16
+AWAY_BATCH = 8
+TAIL_BATCH = 4
 GROUP = ("spec", "line")
 
 HIGH = lax.Precision.HIGHEST
@@ -23,10 +24,29 @@
 VMEM_BYTES = 40 * 1024 * 1024
 
 
-def exchanged(value, start):
-    peers = lax.axis_size(GROUP)
-    pairs = [(i, i + 1) for i in range(start, peers - 1, 2)]
-    return lax.ppermute(value, GROUP, pairs + [(j, i) for i, j in pairs])
+def exchanged(value):
+    pairs = [(i, i ^ 1) for i in range(lax.axis_size(GROUP))]
+    return lax.ppermute(value, GROUP, pairs)
+
+
+def all_layers(own, other, groups):
+    lays = lax.axis_size("lay")
+    members = [
+        [lays * (d % groups) + i for d in (odd, odd + 1) for i in range(lays)]
+        for odd in range(1, groups, 2)
+    ]
+    is_odd = (lax.axis_index(GROUP) & 1) == 1
+    halves = jnp.stack([jnp.where(is_odd, own, other), jnp.where(is_odd, other, own)])
+    copies = jnp.broadcast_to(halves[:, None], (2, lays) + own.shape)
+    landed = lax.all_to_all(
+        copies.reshape((2 * lays,) + own.shape),
+        GROUP + ("lay",),
+        0,
+        0,
+        axis_index_groups=members,
+        tiled=True,
+    )
+    return landed.reshape(copies.shape)
 
 
 def summed_over(copies, total, size, stride):
@@ -80,8 +100,6 @@
     near, press_v, temper_v, offset_v, strength_v, energy_v, lwidth_v, dwidth_v, species_v = vmem
     rate_ref, mix_ref, amp_ref, point_ref, list_ref = scratch[10:15]
     home_acc, away_acc = scratch[15:17], scratch[17:19]
-    home_bufs = scratch[19 : 19 + 2 * HOME_BATCH]
-    away_bufs = home_bufs[: 2 * AWAY_BATCH]
     copies = [pltpu.make_async_copy(s, d, sems.at[i]) for i, (s, d) in enumerate(zip(hbm, vmem))]
     for copy in copies:
         copy.start()
@@ -94,15 +112,12 @@
     group = own_place()[0]
     base = (group - 1) * OWN_TILES
     copies[0].wait()
-    pad = 2 * AWAY_BATCH
-    for k in range(pad):
-        list_ref[k] = jnp.int32(0)
-    found = jnp.int32(pad)
+    found = jnp.int32(0)
     for b in range(blocks):
         for j in range(1, NEAR):
             list_ref[found] = jnp.int32(NEAR * b + j)
             found = found + (near[j, b] >= 0).astype(jnp.int32)
-    for k in range(2 * pad):
+    for k in range(2 * TAIL_BATCH):
         list_ref[found + k] = jnp.int32(0)
 
     for copy in copies[1:]:
@@ -148,11 +163,12 @@
             tile = jnp.where(entry == j, tiles[j], tile)
         return tile
 
-    def evaluate(b, shift, buf, at, split):
+    def evaluate(b, shift, split):
         shape = (16, LBLK)
         shift = jnp.broadcast_to(shift, shape)
         rate = [jnp.broadcast_to(rate_ref[layer, pl.ds(b, 1), :], shape) for layer in range(2)]
         mix = [jnp.broadcast_to(mix_ref[layer, pl.ds(b, 1), :], shape) for layer in range(2)]
+        parts = [[], []]
         for k in range(0, TILE, 16):
             x = point_ref[k : k + 16, :] + shift
             square = x * x
@@ -160,11 +176,11 @@
                 q = square * rate[layer]
                 value = 1.0 / (1.0 - q) + mix[layer] * jnp.exp2(q)
                 high = value.astype(jnp.bfloat16)
-                buf[layer, k : k + 16, at : at + LBLK] = high
                 if split:
-                    buf[layer, k : k + 16, LBLK:] = (value - high.astype(jnp.float32)).astype(
-                        jnp.bfloat16
-                    )
+                    low = (value - high.astype(jnp.float32)).astype(jnp.bfloat16)
+                    high = jnp.concatenate([high, low], axis=1)
+                parts[layer].append(high)
+        return [jnp.concatenate(p, axis=0) for p in parts]
 
     def times(left, right):
         return lax.dot_general(
@@ -174,12 +190,10 @@
     def slot_of(tile, live):
         return jnp.where(live & (tile >= 0), tile - base, slots)
 
-    def home_evaluate(b, buf):
-        evaluate(b, -offset_v[pl.ds(b, 1), :], buf, 0, True)
+    def home_evaluate(b):
+        return evaluate(b, -offset_v[pl.ds(b, 1), :], True)
 
     def home_reduce(b, buf):
-        live = b >= 0
-        b = jnp.maximum(b, 0)
         tiles, _, own = entries(b)
         hit = home_key == own * 8 + species_v[pl.ds(b, 1), :]
         for layer in range(2):
@@ -189,19 +203,21 @@
             left = jnp.where(hit, part, 0.0).astype(jnp.bfloat16)
             sums = times(jnp.concatenate([left, left], axis=1), buf[layer])
             for j in range(NEAR):
-                home_acc[layer][slot_of(tiles[j], live)] += sums[8 * j : 8 * j + 8]
+                home_acc[layer][slot_of(tiles[j], True)] += sums[8 * j : 8 * j + 8]
 
     def decode(i):
         code = list_ref[i]
         return lax.shift_right_logical(code, 2), code & 3
 
-    def away_evaluate(i, buf):
+    def away_evaluate(i):
+        sides = []
         for k in range(2):
             b, r = decode(2 * i + k)
             tiles, count, own = entries(b)
             apart = chosen(rotated(own, count, r), tiles) - chosen(own, tiles)
             shift = (apart * TILE).astype(jnp.float32) - offset_v[pl.ds(b, 1), :]
-            evaluate(b, shift, buf, k * LBLK, False)
+            sides.append(evaluate(b, shift, False))
+        return [jnp.concatenate(both, axis=1) for both in zip(*sides)]
 
     def away_reduce(i, buf):
         items = []
@@ -233,34 +249,21 @@
                     part = jnp.where(upper_half, part, 0.0) if j % 2 else jnp.where(upper_half, 0.0, part)
                     away_acc[layer][slot[j]] += part
 
-    def alternate(batch, bufs, evaluate_one, reduce_one, turns):
+    def in_batches(batch, first, turns, evaluate_one, reduce_one):
         def step(i, carry):
-            at = 2 * batch * i
             for k in range(batch):
-                evaluate_one(at + k, bufs[k])
-            for k in range(batch):
-                reduce_one(at - batch + k, bufs[batch + k])
-            for k in range(batch):
-                evaluate_one(at + batch + k, bufs[batch + k])
-            for k in range(batch):
-                reduce_one(at + k, bufs[k])
+                at = first + batch * i + k
+                reduce_one(at, evaluate_one(at))
             return carry
 
         lax.fori_loop(0, turns, step, 0)
-        for k in range(batch):
-            reduce_one(2 * batch * turns - batch + k, bufs[batch + k])
-
-    alternate(
-        HOME_BATCH, home_bufs, home_evaluate, home_reduce, jnp.int32(blocks // (2 * HOME_BATCH))
-    )
-    span = 4 * AWAY_BATCH
-    alternate(
-        AWAY_BATCH,
-        away_bufs,
-        lambda i, buf: away_evaluate(i + AWAY_BATCH, buf),
-        lambda i, buf: away_reduce(i + AWAY_BATCH, buf),
-        lax.div(found - pad + span - 1, span),
-    )
+
+    in_batches(HOME_BATCH, 0, blocks // HOME_BATCH, home_evaluate, home_reduce)
+    units = lax.shift_right_logical(found + 1, 1)
+    full = lax.div(units, AWAY_BATCH)
+    in_batches(AWAY_BATCH, 0, full, away_evaluate, away_reduce)
+    rest = lax.div(units - AWAY_BATCH * full + TAIL_BATCH - 1, TAIL_BATCH)
+    in_batches(TAIL_BATCH, AWAY_BATCH * full, rest, away_evaluate, away_reduce)
 
     even = (group & 1) == 0
     for slot in range(OWN_TILES):
@@ -303,18 +306,28 @@
             f32((2,) + block_shape),
             f32((2,) + block_shape),
             f32((TILE, LBLK)),
-            pltpu.SMEM((blocks * (NEAR - 1) + 6 * AWAY_BATCH,), jnp.int32),
+            pltpu.SMEM((blocks * (NEAR - 1) + 2 * TAIL_BATCH,), jnp.int32),
         ]
-        + [f32((3 * OWN_TILES + 1, 8, TILE))] * 4
-        + [pltpu.VMEM((2, TILE, 2 * LBLK), jnp.bfloat16)] * (2 * HOME_BATCH),
+        + [f32((3 * OWN_TILES + 1, 8, TILE))] * 4,
         name="pair_sums",
     )(near, press.reshape(1, 2), temper.reshape(1, 2), *[v.reshape(block_shape) for v in lines])
 
 
 def amounts_kernel(
-    points, index_ref, table_ref, noise_ref, sums_ref, amounts_ref, factor_ref, scale_ref, out_ref
+    points,
+    index_ref,
+    table_ref,
+    noise_ref,
+    own_ref,
+    other_ref,
+    amounts_ref,
+    factor_ref,
+    scale_ref,
+    own_out,
+    other_out,
 ):
-    out_ref[...] = sums_ref[...]
+    own_out[...] = own_ref[...]
+    other_out[...] = other_ref[...]
     scale_ref[...] = (1.0 / points) / noise_ref[...]
     layers, sounds = index_ref.shape
     kinds, entries = table_ref.shape
@@ -331,7 +344,7 @@
         factor_ref[a] = amounts * amounts_ref[pl.ds(first + a, 1), :]
 
 
-def amount_tables(points, index, table, noise, sums):
+def amount_tables(points, index, table, noise, own, other):
     layers, sounds = index.shape
     columns = layers * SPECIES
     vmem = pl.BlockSpec(memory_space=pltpu.VMEM)
@@ -341,19 +354,20 @@
             jax.ShapeDtypeStruct((columns, sounds), jnp.float32),
             jax.ShapeDtypeStruct((2 * SPECIES, columns, sounds), jnp.float32),
             jax.ShapeDtypeStruct((1, noise.shape[0]), jnp.float32),
-            jax.ShapeDtypeStruct(sums.shape, jnp.float32),
+            jax.ShapeDtypeStruct(own.shape, jnp.float32),
+            jax.ShapeDtypeStruct(other.shape, jnp.float32),
         ),
-        in_specs=[vmem] * 4,
-        out_specs=[vmem] * 4,
+        in_specs=[vmem] * 5,
+        out_specs=[vmem] * 5,
         compiler_params=pltpu.CompilerParams(vmem_limit_bytes=VMEM_BYTES),
         cost_estimate=pl.CostEstimate(flops=2_000_000, bytes_accessed=100_000, transcendentals=0),
         name="amount_tables",
-    )(index, table, noise.reshape(1, -1), sums)
+    )(index, table, noise.reshape(1, -1), own, other)
 
 
 def gram_kernel(all_ref, amounts_ref, factor_ref, scale_ref, transmit_ref, out_ref):
-    lays, own = all_ref.shape[:2]
-    cross = jnp.concatenate([all_ref[i] for i in range(lays)], axis=0)
+    lays, own = all_ref.shape[1:3]
+    cross = jnp.concatenate([all_ref[0, i] + all_ref[1, i] for i in range(lays)], axis=0)
     depth = lax.dot_general(
         amounts_ref[...],
         cross,
@@ -365,8 +379,9 @@
     transmit_ref[...] = passed
     weight = passed * passed * scale_ref[...]
     lay = own_place()[1]
+    mine = all_ref[0, lay] + all_ref[1, lay]
     for a in range(own):
-        scaled = weight * all_ref[lay, a : a + 1, :]
+        scaled = weight * mine[a : a + 1, :]
         gram = lax.dot_general(
             cross,
             scaled,
@@ -418,13 +433,12 @@
         line_species,
     )
     first, middle, second = pair_sums(cutoff.T, layer_pressure, layer_temp, lines)
-    landed = [exchanged(first, 0), exchanged(second, 1)]
+    landed = exchanged(first)
     points = noise_var.shape[0] * groups
-    amounts, factor, scale, middle = amount_tables(
-        points, column_index.T, column_table, noise_var, middle
-    )
-    cross_own = middle + landed[0] + landed[1]
-    cross_all = lax.all_gather(cross_own, "lay", axis=0)
+    amounts, factor, scale, middle, second = amount_tables(
+        points, column_index.T, column_table, noise_var, middle, second
+    )
+    cross_all = all_layers(middle + landed, second, groups)
     transmit, partial = gram_parts(cross_all, amounts, factor, scale)
     flat = partial.reshape(-1, 128)
     stride = 1

time: 63 us -> 59.4 us (0.943)
  Pallas kernels: 15 us -> 12.2 us
  local copies, waits for them, and re-layouts: 1.6 us -> 3.08 us
  waiting for transfers between devices: 1.63 us -> 0.74 us
  blocking collectives: 41.7 us -> 40.9 us
    all_to_all x0 -> x1, blocking collectives: none -> 16.2 us  [all_layers(): lax.all_to_all(copies.reshape((2 * lays,) + own.shape), GROUP + ('lay',),...]
    all_to_all x2, blocking collectives: 34.8 us -> 24.6 us  [summed_over(): lax.all_to_all(copies, GROUP, 0, 0, axis_index_groups=members, tiled=True)]
    all_gather x1 -> x0, blocking collectives: 6.93 us -> none  [body(): cross_all = lax.all_gather(cross_own, 'lay', axis=0)]
    pallas_call x1, Pallas kernels: 13.7 us -> 10.9 us  [pair_sums(): pl.pallas_call(pairs_kernel, out_shape=(sums,) * 3, in_specs=[hbm] * 9, o...]
    unnamed x8 -> x10, local copies, waits for them, and re-layouts: 0.77 us -> 2.23 us
    ppermute x2 -> x1, waiting for transfers between devices: 1.63 us -> 0.74 us  [exchanged(): return lax.ppermute(value, GROUP, pairs)]
    ppermute x2 -> x1, starting transfers between devices: 1.46 us -> 0.91 us  [exchanged(): return lax.ppermute(value, GROUP, pairs)]
  transfers between devices with their start and end apart: 2 -> 1, of which waited for: 1 -> 1; matrix products, arithmetic and copies ran while one was open for 0% -> 0% of each run, Pallas kernels for 1% -> 1%
where the time goes in v4:
time: 59.4 us; the launch traced here: 58.6 us
  blocking collectives  40.9 us (69%)
  Pallas kernels  12.2 us (21%)
  local copies, waits for them, and re-layouts  3.08 us (5%)
  starting transfers between devices  0.91 us (2%)
  waiting for transfers between devices  0.74 us (1%)
  between operations  0.7 us (1%)
    all_to_all x2, blocking collectives, summed_over(): lax.all_to_all(copies, GROUP, 0, 0, axis_index_groups=members, tiled=True)  24.6 us
    all_to_all x1, blocking collectives, all_layers(): lax.all_to_all(copies.reshape((2 * lays,) + own.shape), GROUP + ('lay',),...  16.2 us
    pallas_call x1, Pallas kernels, pair_sums(): pl.pallas_call(pairs_kernel, out_shape=(sums,) * 3, in_specs=[hbm] * 9, o...  10.9 us
    unnamed x10, local copies, waits for them, and re-layouts  2.23 us
  transfers between devices with their start and end apart: 1, of which 1 were waited for; matrix products, arithmetic and copies ran while one was open for 0% of the time, Pallas kernels for 1%

profile of v4, /device:TPU:4, one launch (start us, length us, event | category | flops | bytes accessed | tf_op | source)
XLA Modules:
  0.0 58.6 jit_solution(7873404182507278630)
XLA Ops:
  0.6 10.9 %pair_sums.1 = (f32[6,1024]{1,0:T(8,128)}, f32[6,1024]{1,0:T(8,128)}, f32[6,1024]{1,0:T(8,128)}) custom-call(s32[4,32]{1,0:T(4,128)} %bitcast.29, f32[1,2]{1,0:T(1,128)} %bitcast.30, f32[1,2]{1,0:T(1,128)} %bitcast.31, f32[32,128]{1,0:T(8,128)} %bitcast.23, f32[32,128]{1,0:T(8,128)} %bitcast.24, f32[32,128]{1,0:T(8,128)} %bitcast.25, f32[32,128]{1,0:T(8,128)} %bitcast.26, ...), custom_call_target="tpu_custom_call" | custom-call | tf_op jit(solution)/shard_map/pair_sums/pallas_call | solution.py:295
  11.5 0.9 %collective-permute-start = (f32[6,1024]{1,0:T(8,128)}, f32[6,1024]{1,0:T(8,128)S(1)}, u32[]{:S(2)}, u32[]{:S(2)}) collective-permute-start(f32[6,1024]{1,0:T(8,128)} %get-tuple-element.15), channel_id=1, source_target_pairs={{0,4},{4,0},{8,12},{12,8},{16,20},{20,16},{24,28},{28,24},{32,36},... | collective-permute-start | bytes 73736 | tf_op jit(solution)/shard_map/ppermute | solution.py:29
  12.4 0.0 copy-start.4
  12.4 0.0 copy-start.3
  12.4 0.0 copy-start.2
  12.5 0.7 %copy-done.4 = f32[3,64]{1,0:T(4,128)S(1)} copy-done((f32[3,64]{1,0:T(4,128)S(1)}, f32[3,64]{1,0:T(4,128)}, u32[]{:S(2)}) %copy-start.4) | copy-done | bytes 792
  13.1 0.0 copy-done.3
  13.1 0.0 copy-done.2
  13.2 0.0 copy-start
  13.2 0.8 %copy-done = f32[6,1024]{1,0:T(8,128)S(1)} copy-done((f32[6,1024]{1,0:T(8,128)S(1)}, f32[6,1024]{1,0:T(8,128)}, u32[]{:S(2)}) %copy-start) | copy-done | bytes 24600
  13.9 0.0 copy-start.1
  13.9 0.8 %copy-done.1 = f32[6,1024]{1,0:T(8,128)S(1)} copy-done((f32[6,1024]{1,0:T(8,128)S(1)}, f32[6,1024]{1,0:T(8,128)}, u32[]{:S(2)}) %copy-start.1) | copy-done | bytes 24600
  14.7 0.3 amount_tables.1
  15.0 0.7 %collective-permute-done = f32[6,1024]{1,0:T(8,128)S(1)} collective-permute-done((f32[6,1024]{1,0:T(8,128)}, f32[6,1024]{1,0:T(8,128)S(1)}, u32[]{:S(2)}, u32[]{:S(2)}) %collective-permute-start) | collective-permute-done | bytes 24608 | tf_op jit(solution)/shard_map/ppermute | solution.py:29
  15.8 16.2 %all_to_all.15 = f32[8,6,1024]{2,1,0:T(8,128)S(1)} all-to-all(f32[8,6,1024]{2,1,0:T(8,128)S(1)} %bitcast.21), channel_id=1, replica_groups={{4,5,6,7,8,9,10,11},{12,13,14,15,16,17,18,19},{20,21,22,23,24,25,26,27}..., dimensions={0} | all-to-all | bytes 393216 | tf_op jit(solution)/shard_map/all_to_all | solution.py:41
  32.0 1.0 %gram_parts.1 = (f32[32,1024]{1,0:T(8,128)}, f32[6,24,32]{2,1,0:T(8,128)S(1)}) custom-call(f32[2,4,6,1024]{3,2,1,0:T(8,128)S(1)} %bitcast.18, f32[24,32]{1,0:T(8,128)S(1)} %get-tuple-element.17.amounts_ref, f32[6,24,32]{2,1,0:T(8,128)S(1)} %get-tuple-element.18.factor_ref, f32[1,1024]{1,0:T(1,128)S(1)} %get-tuple-element.19.scale_ref), custom_call_target="tpu_custom_call" | custom-call | tf_op jit(solution)/shard_map/gram_parts/pallas_call | solution.py:399
  33.0 0.1 broadcast_in_dim.9
  33.1 9.2 %all_to_all.16 = f32[8,36,128]{2,1,0:T(8,128)S(1)} all-to-all(f32[8,36,128]{2,1,0:T(8,128)S(1)} %broadcast_in_dim.10), channel_id=1, replica_groups={{0,4,8,12,16,20,24,28},{32,36,40,44,48,52,56,60},{64,68,72,76,80,84,88,..., dimensions={0} | all-to-all | bytes 294912 | tf_op jit(solution)/shard_map/all_to_all | solution.py:58
  42.3 15.5 %all_to_all.17 = f32[8,36,128]{2,1,0:T(8,128)S(1)} all-to-all(f32[8,36,128]{2,1,0:T(8,128)S(1)} %broadcast_in_dim.22), channel_id=1, replica_groups={{0,32,64,96,128,160,192,224},{4,36,68,100,132,164,196,228},{8,40,72,104..., dimensions={0} | all-to-all | bytes 294912 | tf_op jit(solution)/shard_map/all_to_all | solution.py:58
  57.8 0.7 %reshape.54 = f32[6,24,32]{2,1,0:T(8,128)} reshape(f32[36,128]{1,0:T(8,128)S(1)} %reduce_sum.19) | data formatting | bytes 36864 | tf_op jit(solution)/shard_map/reshape | solution.py:450
  (7 shorter events, 0.1 us)
Async XLA Ops:
  11.5 4.2 %collective-permute-start = (f32[6,1024]{1,0:T(8,128)}, f32[6,1024]{1,0:T(8,128)S(1)}, u32[]{:S(2)}, u32[]{:S(2)}) collective-permute-start(f32[6,1024]{1,0:T(8,128)} %get-tuple-element.15), channel_id=1, source_target_pairs={{0,4},{4,0},{8,12},{12,8},{16,20},{20,16},{24,28},{28,24},{32,36},... | collective-permute-start | bytes 73736 | tf_op jit(solution)/shard_map/ppermute | solution.py:29
  12.4 0.7 %copy-start.4 = (f32[3,64]{1,0:T(4,128)S(1)}, f32[3,64]{1,0:T(4,128)}, u32[]{:S(2)}) copy-start(f32[3,64]{1,0:T(4,128)} %table_ref.1) | copy-start | bytes 2308
  12.4 0.7 %copy-start.3 = (f32[1024]{0:T(1024)S(1)}, f32[1024]{0:T(1024)}, u32[]{:S(2)}) copy-start(f32[1024]{0:T(1024)} %param.23) | copy-start | bytes 12292
  12.4 0.7 %copy-start.2 = (s32[32,8]{0,1:T(8,128)S(1)}, s32[32,8]{0,1:T(8,128)}, u32[]{:S(2)}) copy-start(s32[32,8]{0,1:T(8,128)} %param.21) | copy-start | bytes 3076
  13.2 0.8 %copy-start = (f32[6,1024]{1,0:T(8,128)S(1)}, f32[6,1024]{1,0:T(8,128)}, u32[]{:S(2)}) copy-start(f32[6,1024]{1,0:T(8,128)} %get-tuple-element.12.own_ref) | copy-start | bytes 73732
  13.9 0.8 %copy-start.1 = (f32[6,1024]{1,0:T(8,128)S(1)}, f32[6,1024]{1,0:T(8,128)}, u32[]{:S(2)}) copy-start(f32[6,1024]{1,0:T(8,128)} %get-tuple-element.13.other_ref) | copy-start | bytes 73732

commit v5 on v4

--- a/solution.py
+++ b/solution.py
@@ -13,7 +13,8 @@
 NEAR = 4
 SPECIES = 3
 OWN_TILES = 4
-HOME_BATCH = 16
+ROWS = 2 * SPECIES
+HOME_BATCH = 32
 AWAY_BATCH = 8
 TAIL_BATCH = 4
 GROUP = ("spec", "line")
@@ -112,14 +113,6 @@
     group = own_place()[0]
     base = (group - 1) * OWN_TILES
     copies[0].wait()
-    found = jnp.int32(0)
-    for b in range(blocks):
-        for j in range(1, NEAR):
-            list_ref[found] = jnp.int32(NEAR * b + j)
-            found = found + (near[j, b] >= 0).astype(jnp.int32)
-    for k in range(2 * TAIL_BATCH):
-        list_ref[found + k] = jnp.int32(0)
-
     for copy in copies[1:]:
         copy.wait()
     line_tables(
@@ -258,7 +251,18 @@
 
         lax.fori_loop(0, turns, step, 0)
 
-    in_batches(HOME_BATCH, 0, blocks // HOME_BATCH, home_evaluate, home_reduce)
+    def home_step(i, found):
+        for k in range(HOME_BATCH):
+            b = HOME_BATCH * i + k
+            home_reduce(b, home_evaluate(b))
+            for j in range(1, NEAR):
+                list_ref[found] = NEAR * b + j
+                found = found + (near[j, b] >= 0).astype(jnp.int32)
+        return found
+
+    found = lax.fori_loop(0, blocks // HOME_BATCH, home_step, jnp.int32(0))
+    for k in range(2 * TAIL_BATCH):
+        list_ref[found + k] = jnp.int32(0)
     units = lax.shift_right_logical(found + 1, 1)
     full = lax.div(units, AWAY_BATCH)
     in_batches(AWAY_BATCH, 0, full, away_evaluate, away_reduce)
@@ -267,7 +271,6 @@
 
     even = (group & 1) == 0
     for slot in range(OWN_TILES):
-        at = slot * TILE
         for layer in range(2):
             parts = []
             for third in range(3):
@@ -278,20 +281,23 @@
                     + home[SPECIES : 2 * SPECIES]
                     + (away[:SPECIES] + away[4 : 4 + SPECIES])
                 )
-            where = (slice(SPECIES * layer, SPECIES * (layer + 1)), slice(at, at + TILE))
-            outs[0][where] = jnp.where(even, parts[2], parts[0])
-            outs[1][where] = parts[1]
-            outs[2][where] = jnp.where(even, parts[0], parts[2])
+            for half in range(TILE // LBLK):
+                lanes = slice(half * LBLK, (half + 1) * LBLK)
+                piece = [part[:, lanes] for part in parts]
+                start = (2 * slot + half) * ROWS + SPECIES * layer
+                where = slice(start, start + SPECIES)
+                outs[0][where, :] = jnp.where(even, piece[2], piece[0])
+                outs[1][where, :] = piece[1]
+                outs[2][where, :] = jnp.where(even, piece[0], piece[2])
 
 
 def pair_sums(near, press, temper, lines):
     blocks = near.shape[1]
-    row_count = 2 * SPECIES
     vmem = pl.BlockSpec(memory_space=pltpu.VMEM)
     hbm = pl.BlockSpec(memory_space=pltpu.HBM)
     block_shape = (blocks, LBLK)
     f32 = functools.partial(pltpu.VMEM, dtype=jnp.float32)
-    sums = jax.ShapeDtypeStruct((row_count, OWN_TILES * TILE), jnp.float32)
+    sums = jax.ShapeDtypeStruct((ROWS * OWN_TILES * TILE // LBLK, LBLK), jnp.float32)
     return pl.pallas_call(
         pairs_kernel,
         out_shape=(sums,) * 3,
@@ -366,8 +372,12 @@
 
 
 def gram_kernel(all_ref, amounts_ref, factor_ref, scale_ref, transmit_ref, out_ref):
-    lays, own = all_ref.shape[1:3]
-    cross = jnp.concatenate([all_ref[0, i] + all_ref[1, i] for i in range(lays)], axis=0)
+    lays = all_ref.shape[1]
+    cuts = range(0, all_ref.shape[2], ROWS)
+    parts = [all_ref[0, i] + all_ref[1, i] for i in range(lays)]
+    cross = jnp.concatenate(
+        [jnp.concatenate([p[c : c + ROWS] for p in parts], axis=0) for c in cuts], axis=1
+    )
     depth = lax.dot_general(
         amounts_ref[...],
         cross,
@@ -380,7 +390,8 @@
     weight = passed * passed * scale_ref[...]
     lay = own_place()[1]
     mine = all_ref[0, lay] + all_ref[1, lay]
-    for a in range(own):
+    mine = jnp.concatenate([mine[c : c + ROWS] for c in cuts], axis=1)
+    for a in range(ROWS):
         scaled = weight * mine[a : a + 1, :]
         gram = lax.dot_general(
             cross,

time: 59.4 us -> 58.3 us (0.981)
  Pallas kernels: 12.2 us -> 10.8 us
  starting transfers between devices: 0.91 us -> 2.24 us
  local copies, waits for them, and re-layouts: 3.08 us -> 2.28 us
    pallas_call x1, Pallas kernels: 10.9 us -> 9.44 us  [pair_sums(): pl.pallas_call(pairs_kernel, out_shape=(sums,) * 3, in_specs=[hbm] * 9, o...]
    ppermute x1, starting transfers between devices: 0.91 us -> 2.24 us  [exchanged(): return lax.ppermute(value, GROUP, pairs)]
    all_to_all x1, blocking collectives: 16.2 us -> 17.3 us  [all_layers(): lax.all_to_all(copies.reshape((2 * lays,) + own.shape), GROUP + ('lay',),...]
    unnamed x10, local copies, waits for them, and re-layouts: 2.23 us -> 1.44 us
where the time goes in v5:
time: 58.3 us; the launch traced here: 57.6 us
  blocking collectives  41.3 us (71%)
  Pallas kernels  10.8 us (19%)
  local copies, waits for them, and re-layouts  2.28 us (4%)
  starting transfers between devices  2.24 us (4%)
  between operations  0.71 us (1%)
    all_to_all x2, blocking collectives, summed_over(): lax.all_to_all(copies, GROUP, 0, 0, axis_index_groups=members, tiled=True)  24.1 us
    all_to_all x1, blocking collectives, all_layers(): lax.all_to_all(copies.reshape((2 * lays,) + own.shape), GROUP + ('lay',),...  17.3 us
    pallas_call x1, Pallas kernels, pair_sums(): pl.pallas_call(pairs_kernel, out_shape=(sums,) * 3, in_specs=[hbm] * 9, o...  9.44 us
    ppermute x1, starting transfers between devices, exchanged(): return lax.ppermute(value, GROUP, pairs)  2.24 us
    unnamed x10, local copies, waits for them, and re-layouts  1.44 us
  transfers between devices with their start and end apart: 1, of which 1 were waited for; matrix products, arithmetic and copies ran while one was open for 0% of the time, Pallas kernels for 1%

profile of v5, /device:TPU:4, one launch (start us, length us, event | category | flops | bytes accessed | tf_op | source)
XLA Modules:
  0.0 57.6 jit_solution(4504094350648136778)
XLA Ops:
  0.6 0.0 copy-start.3
  0.6 9.4 %pair_sums.1 = (f32[48,128]{1,0:T(8,128)}, f32[48,128]{1,0:T(8,128)}, f32[48,128]{1,0:T(8,128)}) custom-call(s32[4,32]{1,0:T(4,128)} %bitcast.29, f32[1,2]{1,0:T(1,128)} %bitcast.30, f32[1,2]{1,0:T(1,128)} %bitcast.31, f32[32,128]{1,0:T(8,128)} %bitcast.23, f32[32,128]{1,0:T(8,128)} %bitcast.24, f32[32,128]{1,0:T(8,128)} %bitcast.25, f32[32,128]{1,0:T(8,128)} %bitcast.26, ...), custom_call_target="tpu_custom_call" | custom-call | tf_op jit(solution)/shard_map/pair_sums/pallas_call | solution.py:301
  10.1 0.0 copy-start
  10.1 2.2 %collective-permute-start = (f32[48,128]{1,0:T(8,128)}, f32[48,128]{1,0:T(8,128)S(1)}, u32[]{:S(2)}, u32[]{:S(2)}) collective-permute-start(f32[48,128]{1,0:T(8,128)} %get-tuple-element.15), channel_id=1, source_target_pairs={{0,4},{4,0},{8,12},{12,8},{16,20},{20,16},{24,28},{28,24},{32,36},... | collective-permute-start | bytes 73736 | tf_op jit(solution)/shard_map/ppermute | solution.py:30
  12.3 0.0 copy-start.2
  12.3 0.0 copy-start.4
  12.3 0.0 copy-done.3
  12.3 0.0 copy-done
  12.4 0.7 %copy-done.2 = s32[32,8]{0,1:T(8,128)S(1)} copy-done((s32[32,8]{0,1:T(8,128)S(1)}, s32[32,8]{0,1:T(8,128)}, u32[]{:S(2)}) %copy-start.2) | copy-done | bytes 1048
  13.0 0.0 copy-done.4
  13.0 0.0 copy-start.1
  13.0 0.7 %copy-done.1 = f32[48,128]{1,0:T(8,128)S(1)} copy-done((f32[48,128]{1,0:T(8,128)S(1)}, f32[48,128]{1,0:T(8,128)}, u32[]{:S(2)}) %copy-start.1) | copy-done | bytes 24600
  13.8 0.3 amount_tables.1
  14.1 0.3 collective-permute-done
  14.4 17.3 %all_to_all.15 = f32[8,48,128]{2,1,0:T(8,128)S(1)} all-to-all(f32[8,48,128]{2,1,0:T(8,128)S(1)} %bitcast.21), channel_id=1, replica_groups={{4,5,6,7,8,9,10,11},{12,13,14,15,16,17,18,19},{20,21,22,23,24,25,26,27}..., dimensions={0} | all-to-all | bytes 393216 | tf_op jit(solution)/shard_map/all_to_all | solution.py:42
  31.7 1.0 %gram_parts.1 = (f32[32,1024]{1,0:T(8,128)}, f32[6,24,32]{2,1,0:T(8,128)S(1)}) custom-call(f32[2,4,48,128]{3,2,1,0:T(8,128)S(1)} %bitcast.18, f32[24,32]{1,0:T(8,128)S(1)} %get-tuple-element.17.amounts_ref, f32[6,24,32]{2,1,0:T(8,128)S(1)} %get-tuple-element.18.factor_ref, f32[1,1024]{1,0:T(1,128)S(1)} %get-tuple-element.19.scale_ref), custom_call_target="tpu_custom_call" | custom-call | tf_op jit(solution)/shard_map/gram_parts/pallas_call | solution.py:410
  32.7 0.1 broadcast_in_dim.9
  32.8 9.2 %all_to_all.16 = f32[8,36,128]{2,1,0:T(8,128)S(1)} all-to-all(f32[8,36,128]{2,1,0:T(8,128)S(1)} %broadcast_in_dim.10), channel_id=1, replica_groups={{0,4,8,12,16,20,24,28},{32,36,40,44,48,52,56,60},{64,68,72,76,80,84,88,..., dimensions={0} | all-to-all | bytes 294912 | tf_op jit(solution)/shard_map/all_to_all | solution.py:59
  42.0 14.9 %all_to_all.17 = f32[8,36,128]{2,1,0:T(8,128)S(1)} all-to-all(f32[8,36,128]{2,1,0:T(8,128)S(1)} %broadcast_in_dim.22), channel_id=1, replica_groups={{0,32,64,96,128,160,192,224},{4,36,68,100,132,164,196,228},{8,40,72,104..., dimensions={0} | all-to-all | bytes 294912 | tf_op jit(solution)/shard_map/all_to_all | solution.py:59
  56.9 0.7 %reshape.54 = f32[6,24,32]{2,1,0:T(8,128)} reshape(f32[36,128]{1,0:T(8,128)S(1)} %reduce_sum.19) | data formatting | bytes 36864 | tf_op jit(solution)/shard_map/reshape | solution.py:461
  (7 shorter events, 0.1 us)
Async XLA Ops:
  0.6 11.7 %copy-start.3 = (f32[1024]{0:T(1024)S(1)}, f32[1024]{0:T(1024)}, u32[]{:S(2)}) copy-start(f32[1024]{0:T(1024)} %param.23) | copy-start | bytes 12292
  10.1 2.3 %copy-start = (f32[48,128]{1,0:T(8,128)S(1)}, f32[48,128]{1,0:T(8,128)}, u32[]{:S(2)}) copy-start(f32[48,128]{1,0:T(8,128)} %get-tuple-element.12.own_ref) | copy-start | bytes 73732
  10.1 4.3 %collective-permute-start = (f32[48,128]{1,0:T(8,128)}, f32[48,128]{1,0:T(8,128)S(1)}, u32[]{:S(2)}, u32[]{:S(2)}) collective-permute-start(f32[48,128]{1,0:T(8,128)} %get-tuple-element.15), channel_id=1, source_target_pairs={{0,4},{4,0},{8,12},{12,8},{16,20},{20,16},{24,28},{28,24},{32,36},... | collective-permute-start | bytes 73736 | tf_op jit(solution)/shard_map/ppermute | solution.py:30
  12.3 0.7 %copy-start.2 = (s32[32,8]{0,1:T(8,128)S(1)}, s32[32,8]{0,1:T(8,128)}, u32[]{:S(2)}) copy-start(s32[32,8]{0,1:T(8,128)} %param.21) | copy-start | bytes 3076
  12.3 0.7 %copy-start.4 = (f32[3,64]{1,0:T(4,128)S(1)}, f32[3,64]{1,0:T(4,128)}, u32[]{:S(2)}) copy-start(f32[3,64]{1,0:T(4,128)} %table_ref.1) | copy-start | bytes 2308
  13.0 0.7 %copy-start.1 = (f32[48,128]{1,0:T(8,128)S(1)}, f32[48,128]{1,0:T(8,128)}, u32[]{:S(2)}) copy-start(f32[48,128]{1,0:T(8,128)} %get-tuple-element.13.other_ref) | copy-start | bytes 73732

commit v6 on v5

--- a/solution.py
+++ b/solution.py
@@ -15,8 +15,7 @@
 OWN_TILES = 4
 ROWS = 2 * SPECIES
 HOME_BATCH = 32
-AWAY_BATCH = 8
-TAIL_BATCH = 4
+AWAY_BATCHES = (16, 8, 4)
 GROUP = ("spec", "line")
 
 HIGH = lax.Precision.HIGHEST
@@ -157,13 +156,13 @@
         return tile
 
     def evaluate(b, shift, split):
-        shape = (16, LBLK)
+        shape = (32, LBLK)
         shift = jnp.broadcast_to(shift, shape)
         rate = [jnp.broadcast_to(rate_ref[layer, pl.ds(b, 1), :], shape) for layer in range(2)]
         mix = [jnp.broadcast_to(mix_ref[layer, pl.ds(b, 1), :], shape) for layer in range(2)]
         parts = [[], []]
-        for k in range(0, TILE, 16):
-            x = point_ref[k : k + 16, :] + shift
+        for k in range(0, TILE, 32):
+            x = point_ref[k : k + 32, :] + shift
             square = x * x
             for layer in range(2):
                 q = square * rate[layer]
@@ -261,13 +260,15 @@
         return found
 
     found = lax.fori_loop(0, blocks // HOME_BATCH, home_step, jnp.int32(0))
-    for k in range(2 * TAIL_BATCH):
+    for k in range(2 * AWAY_BATCHES[-1]):
         list_ref[found + k] = jnp.int32(0)
     units = lax.shift_right_logical(found + 1, 1)
-    full = lax.div(units, AWAY_BATCH)
-    in_batches(AWAY_BATCH, 0, full, away_evaluate, away_reduce)
-    rest = lax.div(units - AWAY_BATCH * full + TAIL_BATCH - 1, TAIL_BATCH)
-    in_batches(TAIL_BATCH, AWAY_BATCH * full, rest, away_evaluate, away_reduce)
+    first = jnp.int32(0)
+    for batch in AWAY_BATCHES:
+        spare = batch - 1 if batch == AWAY_BATCHES[-1] else 0
+        turns = lax.div(units - first + spare, batch)
+        in_batches(batch, first, turns, away_evaluate, away_reduce)
+        first = first + batch * turns
 
     even = (group & 1) == 0
     for slot in range(OWN_TILES):
@@ -312,7 +313,7 @@
             f32((2,) + block_shape),
             f32((2,) + block_shape),
             f32((TILE, LBLK)),
-            pltpu.SMEM((blocks * (NEAR - 1) + 2 * TAIL_BATCH,), jnp.int32),
+            pltpu.SMEM((blocks * (NEAR - 1) + 2 * AWAY_BATCHES[-1],), jnp.int32),
         ]
         + [f32((3 * OWN_TILES + 1, 8, TILE))] * 4,
         name="pair_sums",

time: 58.3 us -> 57.9 us (level)
  starting transfers between devices: 2.24 us -> 1.1 us
  waiting for transfers between devices: 0.26 us -> 1.26 us
    ppermute x1, starting transfers between devices: 2.24 us -> 1.1 us  [exchanged(): return lax.ppermute(value, GROUP, pairs)]
    ppermute x1, waiting for transfers between devices: 0.26 us -> 1.26 us  [exchanged(): return lax.ppermute(value, GROUP, pairs)]
    all_to_all x1, blocking collectives: 17.3 us -> 16.3 us  [all_layers(): lax.all_to_all(copies.reshape((2 * lays,) + own.shape), GROUP + ('lay',),...]
    all_to_all x2, blocking collectives: 24.1 us -> 24.7 us  [summed_over(): lax.all_to_all(copies, GROUP, 0, 0, axis_index_groups=members, tiled=True)]
where the time goes in v6:
time: 57.9 us; the launch traced here: 57.5 us
  blocking collectives  40.9 us (71%)
  Pallas kernels  11.2 us (19%)
  local copies, waits for them, and re-layouts  2.28 us (4%)
  waiting for transfers between devices  1.26 us (2%)
  starting transfers between devices  1.1 us (2%)
  between operations  0.71 us (1%)
    all_to_all x2, blocking collectives, summed_over(): lax.all_to_all(copies, GROUP, 0, 0, axis_index_groups=members, tiled=True)  24.7 us
    all_to_all x1, blocking collectives, all_layers(): lax.all_to_all(copies.reshape((2 * lays,) + own.shape), GROUP + ('lay',),...  16.3 us
    pallas_call x1, Pallas kernels, pair_sums(): pl.pallas_call(pairs_kernel, out_shape=(sums,) * 3, in_specs=[hbm] * 9, o...  9.84 us
    unnamed x10, local copies, waits for them, and re-layouts  1.44 us
    ppermute x1, waiting for transfers between devices, exchanged(): return lax.ppermute(value, GROUP, pairs)  1.26 us
  transfers between devices with their start and end apart: 1, of which 1 were waited for; matrix products, arithmetic and copies ran while one was open for 0% of the time, Pallas kernels for 1%

profile of v6, /device:TPU:4, one launch (start us, length us, event | category | flops | bytes accessed | tf_op | source)
XLA Modules:
  0.0 57.5 jit_solution(3989058544241424897)
XLA Ops:
  0.6 0.0 copy-start.3
  0.6 9.8 %pair_sums.1 = (f32[48,128]{1,0:T(8,128)}, f32[48,128]{1,0:T(8,128)}, f32[48,128]{1,0:T(8,128)}) custom-call(s32[4,32]{1,0:T(4,128)} %bitcast.29, f32[1,2]{1,0:T(1,128)} %bitcast.30, f32[1,2]{1,0:T(1,128)} %bitcast.31, f32[32,128]{1,0:T(8,128)} %bitcast.23, f32[32,128]{1,0:T(8,128)} %bitcast.24, f32[32,128]{1,0:T(8,128)} %bitcast.25, f32[32,128]{1,0:T(8,128)} %bitcast.26, ...), custom_call_target="tpu_custom_call" | custom-call | tf_op jit(solution)/shard_map/pair_sums/pallas_call | solution.py:302
  10.5 0.0 copy-start
  10.5 1.1 %collective-permute-start = (f32[48,128]{1,0:T(8,128)}, f32[48,128]{1,0:T(8,128)S(1)}, u32[]{:S(2)}, u32[]{:S(2)}) collective-permute-start(f32[48,128]{1,0:T(8,128)} %get-tuple-element.15), channel_id=1, source_target_pairs={{0,4},{4,0},{8,12},{12,8},{16,20},{20,16},{24,28},{28,24},{32,36},... | collective-permute-start | bytes 73736 | tf_op jit(solution)/shard_map/ppermute | solution.py:29
  11.6 0.0 copy-start.2
  11.6 0.0 copy-start.4
  11.6 0.0 copy-done.3
  11.6 0.0 copy-done
  11.6 0.7 %copy-done.2 = s32[32,8]{0,1:T(8,128)S(1)} copy-done((s32[32,8]{0,1:T(8,128)S(1)}, s32[32,8]{0,1:T(8,128)}, u32[]{:S(2)}) %copy-start.2) | copy-done | bytes 1048
  12.3 0.0 copy-done.4
  12.3 0.0 copy-start.1
  12.3 0.7 %copy-done.1 = f32[48,128]{1,0:T(8,128)S(1)} copy-done((f32[48,128]{1,0:T(8,128)S(1)}, f32[48,128]{1,0:T(8,128)}, u32[]{:S(2)}) %copy-start.1) | copy-done | bytes 24600
  13.0 0.3 amount_tables.1
  13.4 1.3 %collective-permute-done = f32[48,128]{1,0:T(8,128)S(1)} collective-permute-done((f32[48,128]{1,0:T(8,128)}, f32[48,128]{1,0:T(8,128)S(1)}, u32[]{:S(2)}, u32[]{:S(2)}) %collective-permute-start) | collective-permute-done | bytes 24608 | tf_op jit(solution)/shard_map/ppermute | solution.py:29
  14.7 16.3 %all_to_all.15 = f32[8,48,128]{2,1,0:T(8,128)S(1)} all-to-all(f32[8,48,128]{2,1,0:T(8,128)S(1)} %bitcast.21), channel_id=1, replica_groups={{4,5,6,7,8,9,10,11},{12,13,14,15,16,17,18,19},{20,21,22,23,24,25,26,27}..., dimensions={0} | all-to-all | bytes 393216 | tf_op jit(solution)/shard_map/all_to_all | solution.py:41
  30.9 1.0 %gram_parts.1 = (f32[32,1024]{1,0:T(8,128)}, f32[6,24,32]{2,1,0:T(8,128)S(1)}) custom-call(f32[2,4,48,128]{3,2,1,0:T(8,128)S(1)} %bitcast.18, f32[24,32]{1,0:T(8,128)S(1)} %get-tuple-element.17.amounts_ref, f32[6,24,32]{2,1,0:T(8,128)S(1)} %get-tuple-element.18.factor_ref, f32[1,1024]{1,0:T(1,128)S(1)} %get-tuple-element.19.scale_ref), custom_call_target="tpu_custom_call" | custom-call | tf_op jit(solution)/shard_map/gram_parts/pallas_call | solution.py:411
  31.9 0.1 broadcast_in_dim.9
  32.1 9.2 %all_to_all.16 = f32[8,36,128]{2,1,0:T(8,128)S(1)} all-to-all(f32[8,36,128]{2,1,0:T(8,128)S(1)} %broadcast_in_dim.10), channel_id=1, replica_groups={{0,4,8,12,16,20,24,28},{32,36,40,44,48,52,56,60},{64,68,72,76,80,84,88,..., dimensions={0} | all-to-all | bytes 294912 | tf_op jit(solution)/shard_map/all_to_all | solution.py:58
  41.2 15.5 %all_to_all.17 = f32[8,36,128]{2,1,0:T(8,128)S(1)} all-to-all(f32[8,36,128]{2,1,0:T(8,128)S(1)} %broadcast_in_dim.22), channel_id=1, replica_groups={{0,32,64,96,128,160,192,224},{4,36,68,100,132,164,196,228},{8,40,72,104..., dimensions={0} | all-to-all | bytes 294912 | tf_op jit(solution)/shard_map/all_to_all | solution.py:58
  56.8 0.7 %reshape.54 = f32[6,24,32]{2,1,0:T(8,128)} reshape(f32[36,128]{1,0:T(8,128)S(1)} %reduce_sum.19) | data formatting | bytes 36864 | tf_op jit(solution)/shard_map/reshape | solution.py:462
  (7 shorter events, 0.1 us)
Async XLA Ops:
  0.6 11.0 %copy-start.3 = (f32[1024]{0:T(1024)S(1)}, f32[1024]{0:T(1024)}, u32[]{:S(2)}) copy-start(f32[1024]{0:T(1024)} %param.23) | copy-start | bytes 12292
  10.5 1.1 %copy-start = (f32[48,128]{1,0:T(8,128)S(1)}, f32[48,128]{1,0:T(8,128)}, u32[]{:S(2)}) copy-start(f32[48,128]{1,0:T(8,128)} %get-tuple-element.12.own_ref) | copy-start | bytes 73732
  10.5 4.1 %collective-permute-start = (f32[48,128]{1,0:T(8,128)}, f32[48,128]{1,0:T(8,128)S(1)}, u32[]{:S(2)}, u32[]{:S(2)}) collective-permute-start(f32[48,128]{1,0:T(8,128)} %get-tuple-element.15), channel_id=1, source_target_pairs={{0,4},{4,0},{8,12},{12,8},{16,20},{20,16},{24,28},{28,24},{32,36},... | collective-permute-start | bytes 73736 | tf_op jit(solution)/shard_map/ppermute | solution.py:29
  11.6 0.7 %copy-start.2 = (s32[32,8]{0,1:T(8,128)S(1)}, s32[32,8]{0,1:T(8,128)}, u32[]{:S(2)}) copy-start(s32[32,8]{0,1:T(8,128)} %param.21) | copy-start | bytes 3076
  11.6 0.7 %copy-start.4 = (f32[3,64]{1,0:T(4,128)S(1)}, f32[3,64]{1,0:T(4,128)}, u32[]{:S(2)}) copy-start(f32[3,64]{1,0:T(4,128)} %table_ref.1) | copy-start | bytes 2308
  12.3 0.7 %copy-start.1 = (f32[48,128]{1,0:T(8,128)S(1)}, f32[48,128]{1,0:T(8,128)}, u32[]{:S(2)}) copy-start(f32[48,128]{1,0:T(8,128)} %get-tuple-element.13.other_ref) | copy-start | bytes 73732
